TPU v7x, 32 devices: a whole 2x2x4 slice. The times are simulated.
32 devices in a mesh: row: 4 (over y, x), col: 8 (over z, core).
Axes of the slice: x: 2, y: 2, z: 4, core: 2. Of those that a mesh axis runs over, the one named last changes fastest.
Arguments:
- slab: bfloat16 [256, 128, 128], P(('row', 'col')), may hold values from -6 to 6
- pair: bfloat16 [256, 256, 128], P('row', 'col'), may hold values from -6 to 6
- mask: int32 [256], replicated, may hold values 0 or 1
- ln_gain: float32 [128], replicated, may hold values from 0.1 to 1.9
- w_query: bfloat16 [128, 128], replicated, may hold values from -0.5 to 0.5
- w_key: bfloat16 [128, 128], replicated, may hold values from -0.5 to 0.5
- w_value: bfloat16 [128, 128], replicated, may hold values from -0.5 to 0.5
- w_gate: bfloat16 [128, 128], replicated, may hold values from -0.5 to 0.5
- gate_bias: float32 [128], replicated, may hold values from -4 to 4
- w_bias: bfloat16 [128, 4], replicated, may hold values from -24 to 24
- w_out: bfloat16 [128, 128], replicated, may hold values from -0.5 to 0.5
- out_bias: float32 [128], replicated, may hold values from -3 to 3
Outputs:
- update: bfloat16 [256, 128, 128], P(('row', 'col'))
Inputs may be any that keep to these rules, and one draw needn't show every extreme that they name: `mask`: 1 marks a real token, 0 a padding token.
All inputs are finite; a program needn't handle non-finite values.
Results may differ from a plain program's by a relative error of at most 0.01.
The roundings to bfloat16 on the way count: a program that leaves them out, or rounds other values in their place, can miss the bound.
Values may be sent and summed in bfloat16 or wider, within the bound.
A program may use at most 128 MiB of HBM per device.

v0:
```python
import math

import jax
import jax.numpy as jnp
from jax import lax
from jax.sharding import PartitionSpec as P


def normalize(values, ln_gain):
    values = values.astype(jnp.float32)
    center = jnp.mean(values, axis=-1, keepdims=True)
    spread = jnp.mean(jnp.square(values - center), axis=-1, keepdims=True)
    return ((values - center) * lax.rsqrt(spread + 1e-05) * ln_gain).astype(jnp.bfloat16)


def project(rows, weight):
    flat = rows.reshape(-1, rows.shape[-1])
    result = jnp.dot(flat, weight, preferred_element_type=jnp.float32)
    return result.reshape(rows.shape[:-1] + (weight.shape[1],))


def per_device(
    slab, pair, mask, ln_gain, w_query, w_key, w_value, w_gate, gate_bias, w_bias, w_out, out_bias
):
    rows_count = lax.axis_size("row")
    cols_count = lax.axis_size("col")
    tok_blk, width, channels = slab.shape
    heads = w_bias.shape[1]
    head_dim = channels // heads
    scale = 1.0 / math.sqrt(head_dim)
    normed_pair = normalize(pair, ln_gain)
    bias_tile = jnp.einsum(
        "abc,ch->hab", normed_pair, w_bias, preferred_element_type=jnp.float32
    ).astype(jnp.bfloat16)
    mirrored = lax.all_to_all(
        lax.all_to_all(bias_tile, "col", split_axis=1, concat_axis=2, tiled=True),
        "row",
        split_axis=2,
        concat_axis=1,
        tiled=True,
    )
    col_index = lax.axis_index("col")
    mask_grid = mask.reshape(rows_count, cols_count, tok_blk)
    key_mask = lax.dynamic_index_in_dim(mask_grid, col_index, 1, keepdims=False).reshape(-1)
    key_shift = (key_mask.astype(jnp.float32) - 1.0) * 1000000000.0
    normed_own = normalize(slab, ln_gain)
    query_all = project(
        normalize(lax.all_gather(slab, "col", axis=0, tiled=True), ln_gain), w_query
    ).astype(jnp.bfloat16)
    w_joined = jnp.concatenate([w_key, w_value], axis=1)
    joined = project(
        normalize(lax.all_gather(slab, "row", axis=0, tiled=True), ln_gain), w_joined
    ).astype(jnp.bfloat16)
    key_all = joined[..., :channels]
    value_all = joined[..., channels:]
    key_count = key_all.shape[0]
    query_count = query_all.shape[0]
    block_rows = math.gcd(query_count, 64)
    block_count = query_count // block_rows
    query_blocks = query_all.reshape(block_count, block_rows, width, heads, head_dim)
    bias_blocks = jnp.transpose(
        mirrored.reshape(heads, key_count, block_count, block_rows), (2, 3, 0, 1)
    )
    keys_split = key_all.reshape(key_count, width, heads, head_dim)
    values_split = value_all.reshape(key_count, width, heads, head_dim)

    def one_block(inputs):
        query_blk, bias_blk = inputs
        scores = (
            jnp.einsum("ijhd,kjhd->ihjk", query_blk, keys_split, preferred_element_type=jnp.float32)
            * scale
        )
        scores = scores + bias_blk.astype(jnp.float32)[:, :, None, :] + key_shift
        block_top = jnp.max(scores, axis=-1)
        weights = jnp.exp(scores - block_top[..., None])
        block_total = jnp.sum(weights, axis=-1)
        block_acc = jnp.einsum(
            "ihjk,kjhd->ijhd",
            weights.astype(jnp.bfloat16),
            values_split,
            preferred_element_type=jnp.float32,
        )
        return (block_top, block_total, block_acc)

    running = lax.map(one_block, (query_blocks, bias_blocks))
    local_top = running[0].reshape(query_count, heads, width)
    local_total = running[1].reshape(query_count, heads, width)
    local_acc = running[2].reshape(query_count, width, heads, head_dim)
    global_top = lax.pmax(local_top.astype(jnp.bfloat16), "col").astype(local_top.dtype)
    rescale = jnp.exp(local_top - global_top)
    numer = (local_acc * jnp.transpose(rescale, (0, 2, 1))[..., None]).reshape(
        query_count, width, channels
    )
    denom = local_total * rescale
    numer_own, denom_own = (
        lax.psum_scatter(numer.astype(jnp.bfloat16), "col", scatter_dimension=0, tiled=True).astype(
            jnp.float32
        ),
        lax.psum_scatter(denom.astype(jnp.bfloat16), "col", scatter_dimension=0, tiled=True).astype(
            jnp.float32
        ),
    )
    attended = (
        numer_own.reshape(tok_blk, width, heads, head_dim)
        / jnp.transpose(denom_own, (0, 2, 1))[..., None]
    )
    gate = jax.nn.sigmoid(project(normed_own, w_gate) + gate_bias)
    hidden = (gate * attended.reshape(tok_blk, width, channels)).astype(jnp.bfloat16)
    update = project(hidden, w_out) + out_bias
    return update.astype(jnp.bfloat16)


def solution(mesh):
    placed = (
        P(("row", "col"), None, None),
        P("row", "col", None),
        P(),
        P(),
        P(),
        P(),
        P(),
        P(),
        P(),
        P(),
        P(),
        P(),
    )
    return jax.shard_map(
        per_device,
        mesh=mesh,
        in_specs=placed,
        out_specs=P(("row", "col"), None, None),
        check_vma=False,
    )
```

profile of v0, /device:TPU:0, one launch (start us, length us, event | category | flops | bytes accessed | tf_op | source)
XLA Modules:
  0.0 250.1 jit_solution(12942268392038088553)
XLA Ops:
  6.6 0.7 all-gather.3.cloned.1.call-update
  7.3 0.7 all-gather.5.cloned.1.call-update
  8.0 1.4 convert_reduce_fusion.2
  9.4 1.7 fusion.37
  11.1 1.9 fusion.76
  13.2 11.8 %all_to_all.30 = bf16[8,2,512]{2,1,0:T(2,128)(2,1)S(1)} all-to-all(bf16[8,2,512]{2,1,0:T(2,128)(2,1)S(1)} %reshape.141), channel_id=1, replica_groups=mesh['row'=4,'col'=8] {'col'}, dimensions={0} | all-to-all | bytes 32768 | tf_op jit(solution)/shard_map/all_to_all | solution.py:36
  25.3 0.9 reshape.143
  26.2 3.7 %all-to-all-start.1 = ((bf16[4,2,1024]{2,1,0:T(2,128)(2,1)}), bf16[4,2,1024]{2,1,0:T(2,128)(2,1)S(1)}, u32[]{:S(2)}, u32[]{:S(2)}) async-start(bf16[4,2,1024]{2,1,0:T(2,128)(2,1)} %reshape.143), calls=%async_computation.1 | async-start | bytes 32768 | tf_op jit(solution)/shard_map/all_to_all | solution.py:35
  29.9 0.8 reshape.124
  30.8 3.9 %all-to-all-done.1 = bf16[4,2,1024]{2,1,0:T(2,128)(2,1)S(1)} async-done(((bf16[4,2,1024]{2,1,0:T(2,128)(2,1)}), bf16[4,2,1024]{2,1,0:T(2,128)(2,1)S(1)}, u32[]{:S(2)}, u32[]{:S(2)}) %all-to-all-start.1) | async-done | bytes 16416 | tf_op jit(solution)/shard_map/all_to_all | solution.py:35
  35.3 3.4 %all-gather.3.cloned.1.call-done = bf16[32,128,128]{2,1,0:T(8,128)(2,1)} async-done(((bf16[8,128,128]{2,1,0:T(8,128)(2,1)}), bf16[32,128,128]{2,1,0:T(8,128)(2,1)}) %all-gather.3.cloned.1.call-update) | async-done | bytes 1048592 | tf_op jit(solution)/shard_map/all_gather | solution.py:52
  38.7 1.6 convert_reduce_fusion.1
  40.3 2.3 fusion.16
  42.7 2.6 %convolution_convert_fusion = bf16[32,128,256]{2,1,0:T(8,128)(2,1)S(1)} fusion(bf16[32,128,128]{2,1,0:T(8,128)(2,1)} %all-gather.3.cloned.1.call-done, f32[128]{0:T(128)S(1)} %copy-done.5, f32[32,128]{1,0:T(8,128)S(1)} %add_rsqrt_fusion.2, f32[32,128]{1,0:T(8,128)S(1)} %broadcast_multiply_fusion.2, bf16[128,128]{1,0:T(8,128)(2,1)S(1)} %copy-done.3, ...), kind=kOutput, calls=%fused_computation.29 | convolution fusion | flops 272236544 | bytes 3244544 | tf_op jit(solution)/shard_map/dot_general | solution.py:18
  46.5 6.4 %copy.95 = bf16[32,128,4,32]{3,0,1,2:T(8,128)(2,1)} copy(bf16[32,128,4,32]{1,3,2,0:T(8,128)(2,1)S(1)} %bitcast.70) | data formatting | bytes 2097152 | tf_op jit(solution)/shard_map/reshape | solution.py:64
  52.9 3.4 %copy.109 = bf16[32,128,128]{0,2,1:T(8,128)(2,1)} copy(bf16[32,128,128]{2,1,0:T(8,128)(2,1)S(1)} %get-tuple-element.23) | data formatting | bytes 2097152 | tf_op jit(solution)/shard_map/reshape | solution.py:65
  56.2 13.1 %all-gather.5.cloned.1.call-done = bf16[64,128,128]{2,1,0:T(8,128)(2,1)} async-done(((bf16[8,128,128]{2,1,0:T(8,128)(2,1)}), bf16[64,128,128]{2,1,0:T(8,128)(2,1)}) %all-gather.5.cloned.1.call-update) | async-done | bytes 2097168 | tf_op jit(solution)/shard_map/all_gather | solution.py:48
  69.3 2.4 convert_reduce_fusion
  71.7 3.6 %fusion.7 = f32[64,128]{1,0:T(8,128)S(1)} fusion(bf16[64,128,128]{2,1,0:T(8,128)(2,1)} %all-gather.5.cloned.1.call-done, f32[64,128]{1,0:T(8,128)S(1)} %broadcast_multiply_fusion.1), kind=kLoop, calls=%fused_computation.12 | loop fusion | flops 4186112 | bytes 2162688 | tf_op jit(solution)/shard_map/reduce_sum | solution.py:12
  75.3 3.3 %fusion.24 = bf16[64,128,128]{1,2,0:T(8,128)(2,1)S(1)} fusion(bf16[64,128,128]{2,1,0:T(8,128)(2,1)S(1)} %copy-done.1, f32[128]{0:T(128)S(1)} %copy-done.5, f32[64,128]{1,0:T(8,128)S(1)} %add_rsqrt_fusion.1, f32[64,128]{1,0:T(8,128)S(1)} %broadcast_multiply_fusion.1, bf16[128,128]{1,0:T(8,128)(2,1)S(1)} %copy-done), kind=kOutput, calls=%fused_computation.28 | convolution fusion | flops 274726912 | bytes 4293120 | tf_op jit(solution)/shard_map/dot_general | solution.py:18
  78.7 7.6 %copy.96 = bf16[64,128,4,32]{0,3,1,2:T(8,128)(2,1)} copy(bf16[64,128,4,32]{1,3,2,0:T(8,128)(2,1)S(1)} %bitcast.71) | data formatting | bytes 4194304 | tf_op jit(solution)/shard_map/while/body/jit(dynamic_index_in_dim)/squeeze | solution.py:85
  86.3 8.5 %fusion.4 = (f32[64,4,128]{0,2,1:T(8,128)S(1)}, f32[4,128,32,64]{3,2,1,0:T(8,128)}) fusion(f32[32]{0:T(128)S(1)} %mul.120, f32[64,4,32]{0,2,1:T(8,128)S(1)} %bitcast.75, bf16[32,128,4,32]{3,0,1,2:T(8,128)(2,1)} %copy.95, bf16[64,128,4,32]{0,3,1,2:T(8,128)(2,1)} %copy.96), kind=kOutput, calls=%fused_computation.7 | convolution fusion | flops 71270400 | bytes 7504000 | tf_op jit(solution)/shard_map/while/body/eval_jaxpr/ijhd,kjhd->ihjk/dot_general | solution.py:70
  95.8 7.0 %fusion.3 = (bf16[64,4,128,32]{0,3,2,1:T(8,128)(2,1)}, f32[64,4,128]{0,2,1:T(8,128)S(1)}) fusion(f32[4,128,32,64]{3,2,1,0:T(8,128)} %get-tuple-element.38, f32[64,4,128]{0,2,1:T(8,128)S(1)} %get-tuple-element.36, f32[32]{0:T(128)S(1)} %mul.120, f32[64,4,32]{0,2,1:T(8,128)S(1)} %bitcast.76), kind=kLoop, calls=%fused_computation.6 | loop fusion | flops 6258688 | bytes 6586496 | tf_op jit(solution)/shard_map/while/body/eval_jaxpr/convert_element_type | solution.py:79
  102.7 46.7 %all-reduce.4.cloned.1.call-done = bf16[64,4,128]{0,2,1:T(8,128)(2,1)} async-done(((bf16[64,4,128]{0,2,1:T(8,128)(2,1)}), bf16[64,4,128]{0,2,1:T(8,128)(2,1)}) %all-reduce.4.cloned.1.call-update) | async-done | bytes 65552 | tf_op jit(solution)/shard_map/pmax | solution.py:89
  149.4 1.0 fusion.65
  150.6 0.7 copy.106
  151.4 6.6 %fusion = bf16[64,128,4,32]{0,3,2,1:T(8,128)(2,1)} fusion(f32[64,128,4]{0,2,1:T(4,128)S(1)} %copy.103, bf16[32,128,4,32]{0,3,2,1:T(8,128)(2,1)} %bitcast.68, bf16[64,4,128,32]{0,3,2,1:T(8,128)(2,1)} %get-tuple-element.21), kind=kOutput, calls=%fused_computation.1 | convolution fusion | flops 69206016 | bytes 5373952 | tf_op jit(solution)/shard_map/while/body/eval_jaxpr/ihjk,kjhd->ijhd/dot_general | solution.py:77
  158.0 5.7 %copy.105 = bf16[64,128,128]{2,1,0:T(8,128)(2,1)} copy(bf16[64,128,128]{0,2,1:T(8,128)(2,1)} %bitcast.69) | data formatting | bytes 4194304 | tf_op jit(solution)/shard_map/convert_element_type | solution.py:96
  165.6 38.8 %all-reduce.6.cloned.1.call-done = bf16[64,4,128]{2,1,0:T(4,128)(2,1)} async-done(((bf16[64,4,128]{2,1,0:T(4,128)(2,1)}), bf16[64,4,128]{2,1,0:T(4,128)(2,1)}) %all-reduce.6.cloned.1.call-update) | async-done | bytes 65552
  204.3 0.7 convert_bitcast_fusion
  205.3 36.1 %reduce-scatter.2.cloned.1.call-done = bf16[8,128,128]{2,1,0:T(8,128)(2,1)} async-done(((bf16[64,128,128]{2,1,0:T(8,128)(2,1)}), bf16[8,128,128]{2,1,0:T(8,128)(2,1)}) %reduce-scatter.2.cloned.1.call-update) | async-done | bytes 262160 | tf_op jit(solution)/shard_map/reduce_scatter | solution.py:96
  241.4 2.2 fusion.35
  (57 shorter events, 5.2 us)
Async XLA Ops:
  6.5 68.8 %copy-start = (bf16[128,128]{1,0:T(8,128)(2,1)S(1)}, bf16[128,128]{1,0:T(8,128)(2,1)}, u32[]{:S(2)}) copy-start(bf16[128,128]{1,0:T(8,128)(2,1)} %param.16) | copy-start | bytes 98308
  6.5 36.1 %copy-start.5 = (f32[128]{0:T(128)S(1)}, f32[128]{0:T(128)}, u32[]{:S(2)}) copy-start(f32[128]{0:T(128)} %param.15) | copy-start | bytes 1540
  6.5 36.1 %copy-start.4 = (bf16[128,128]{1,0:T(8,128)(2,1)S(1)}, bf16[128,128]{1,0:T(8,128)(2,1)}, u32[]{:S(2)}) copy-start(bf16[128,128]{1,0:T(8,128)(2,1)} %param.17) | copy-start | bytes 98308
  6.5 36.1 %copy-start.3 = (bf16[128,128]{1,0:T(8,128)(2,1)S(1)}, bf16[128,128]{1,0:T(8,128)(2,1)}, u32[]{:S(2)}) copy-start(bf16[128,128]{1,0:T(8,128)(2,1)} %param.18) | copy-start | bytes 98308
  6.5 32.2 %all-gather.3.cloned.1.call-start = ((), (), s32[]{:S(2)}) async-start(), calls=%async_computation.3 | async-start | bytes 1310720 | tf_op jit(solution)/shard_map/all_gather | solution.py:52
  7.3 62.0 %all-gather.5.cloned.1.call-start = ((), (), s32[]{:S(2)}) async-start(), calls=%async_computation.4 | async-start | bytes 2359296 | tf_op jit(solution)/shard_map/all_gather | solution.py:48
  26.2 8.5 %all-to-all-start.1 = ((bf16[4,2,1024]{2,1,0:T(2,128)(2,1)}), bf16[4,2,1024]{2,1,0:T(2,128)(2,1)S(1)}, u32[]{:S(2)}, u32[]{:S(2)}) async-start(bf16[4,2,1024]{2,1,0:T(2,128)(2,1)} %reshape.143), calls=%async_computation.1 | async-start | bytes 32768 | tf_op jit(solution)/shard_map/all_to_all | solution.py:35
  29.9 119.5 %all-reduce.4.cloned.1.call-start = ((), (), s32[]{:S(2)}) async-start(), calls=%async_computation.5 | async-start | bytes 262144 | tf_op jit(solution)/shard_map/pmax | solution.py:89
  69.3 6.0 %copy-start.1 = (bf16[64,128,128]{2,1,0:T(8,128)(2,1)S(1)}, bf16[64,128,128]{2,1,0:T(8,128)(2,1)}, u32[]{:S(2)}) copy-start(bf16[64,128,128]{2,1,0:T(8,128)(2,1)} %all-gather.5.cloned.1.call-done) | copy-start | bytes 6291460
  95.5 108.8 %all-reduce.6.cloned.1.call-start = ((), (), s32[]{:S(2)}) async-start(), calls=%async_computation.7 | async-start | bytes 131072
  151.3 90.0 %reduce-scatter.2.cloned.1.call-start = ((), (), s32[]{:S(2)}) async-start(), calls=%async_computation.6 | async-start | bytes 2359296 | tf_op jit(solution)/shard_map/reduce_scatter | solution.py:96
  158.0 5.7 %copy-start.10 = (u32[32]{0:T(128)S(1)}, u32[32]{0:T(128)}, u32[]{:S(2)}) copy-start(u32[32]{0:T(128)} %constant.64) | copy-start | bytes 388
  158.0 7.0 %copy-start.2 = (bf16[8,128,128]{2,1,0:T(8,128)(2,1)S(1)}, bf16[8,128,128]{2,1,0:T(8,128)(2,1)}, u32[]{:S(2)}) copy-start(bf16[8,128,128]{2,1,0:T(8,128)(2,1)} %param.12) | copy-start | bytes 786436
  158.0 83.3 %copy-start.6 = (bf16[128,128]{1,0:T(8,128)(2,1)S(1)}, bf16[128,128]{1,0:T(8,128)(2,1)}, u32[]{:S(2)}) copy-start(bf16[128,128]{1,0:T(8,128)(2,1)} %param.22) | copy-start | bytes 98308
  158.0 83.3 %copy-start.7 = (bf16[128,128]{1,0:T(8,128)(2,1)S(1)}, bf16[128,128]{1,0:T(8,128)(2,1)}, u32[]{:S(2)}) copy-start(bf16[128,128]{1,0:T(8,128)(2,1)} %param.19) | copy-start | bytes 98308
  158.0 83.3 %copy-start.8 = (f32[128]{0:T(128)S(1)}, f32[128]{0:T(128)}, u32[]{:S(2)}) copy-start(f32[128]{0:T(128)} %param.23) | copy-start | bytes 1540
  158.0 83.3 %copy-start.9 = (f32[128]{0:T(128)S(1)}, f32[128]{0:T(128)}, u32[]{:S(2)}) copy-start(f32[128]{0:T(128)} %param.20) | copy-start | bytes 1540
Sparse Core Ops, SparseCore 0:
  9.2 29.4 all-gather.2
  40.3 28.9 all-gather.4
  95.6 53.7 all-reduce.3
  151.7 52.5 all-reduce.5
  206.5 34.8 reduce-scatter.1
where the time goes:
time: 251 us; the launch traced here: 250 us
  waiting for transfers between devices  143 us (57%)
  local copies, waits for them, and re-layouts  28.9 us (12%)
  matrix products  25.3 us (10%)
  other arithmetic  22.8 us (9%)
  between operations  14.1 us (6%)
  blocking collectives  11.8 us (5%)
  starting transfers between devices  4.09 us (2%)
    pmax x1, waiting for transfers between devices, per_device(): lax.pmax(local_top.astype(jnp.bfloat16), 'col').astype(local_top.dtype)  46.7 us
    unnamed x6, waiting for transfers between devices  40.2 us
    reduce_scatter x1, waiting for transfers between devices, per_device(): lax.psum_scatter(numer.astype(jnp.bfloat16), 'col', scatter_dimension=0,...  36.1 us
    all_gather x1, waiting for transfers between devices, per_device(): lax.all_gather(slab, 'col', axis=0, tiled=True)  13.1 us
    all_to_all x1, blocking collectives, per_device(): lax.all_to_all(bias_tile, 'col', split_axis=1, concat_axis=2, tiled=True)  11.8 us
    dot_general x1, matrix products, one_block(): jnp.einsum('ijhd,kjhd->ihjk', query_blk, keys_split, preferred_element_ty...  8.53 us
    dot_general x3, matrix products, project(): result = jnp.dot(flat, weight, preferred_element_type=jnp.float32)  8.17 us
    reduce_sum x4, other arithmetic, normalize(): spread = jnp.mean(jnp.square(values - center), axis=-1, keepdims=True)  7.95 us
  transfers between devices with their start and end apart: 6, of which 6 were waited for; matrix products, arithmetic and copies ran while one was open for 19% of the time, Pallas kernels for 0%

commit v1 on v0

v1 whole, which is shorter than its diff:
```python
import functools
import math

import jax
import jax.numpy as jnp
from jax import lax
from jax.experimental import pallas as pl
from jax.experimental.pallas import tpu as pltpu
from jax.sharding import PartitionSpec as P

MESH = pl.DeviceIdType.MESH
F32 = jnp.float32
BF16 = jnp.bfloat16
NT = (((1,), (1,)), ((), ()))


def normalize(values, gain):
    center = jnp.mean(values, axis=-1, keepdims=True)
    moved = values - center
    spread = jnp.mean(jnp.square(moved), axis=-1, keepdims=True)
    return moved * lax.rsqrt(spread + 1e-05) * gain


def kernel(
    rows_count,
    cols_count,
    slab_ref,
    pair_ref,
    mask_ref,
    gain_ref,
    wq_ref,
    wk_ref,
    wv_ref,
    wg_ref,
    gate_bias_ref,
    wb_ref,
    wo_ref,
    out_bias_ref,
    out_ref,
    slab_f32,
    pair_f32,
    slab_send,
    slab_recv,
    bias,
    chunk_f32,
    query,
    key,
    value_t,
    gate,
    shift,
    back_send,
    back_recv,
    slab_ss,
    slab_rs,
    bias_ss,
    bias_rs,
    relay_ss,
    back_ss,
    back_rs,
):
    devices = rows_count * cols_count
    tok, width, channels = slab_ref.shape
    key_blk, query_blk, _ = pair_ref.shape
    heads = wb_ref.shape[1]
    head_dim = channels // heads
    cols = width // devices
    tokens = devices * tok
    lanes = heads * query_blk
    owners = query_blk // tok
    scale = 1.0 / math.sqrt(head_dim)
    my_row, my_col = lax.axis_index("row"), lax.axis_index("col")
    me = my_row * cols_count + my_col
    sibling = me + 1 - 2 * lax.rem(my_col, 2)
    cores = 2

    def place(p):
        return (p // cols_count, lax.rem(p, cols_count))

    barrier = pltpu.get_barrier_semaphore()

    def greet(n, carry):
        p = lax.rem(me + n, devices)
        pl.semaphore_signal(barrier, inc=1, device_id=place(p), device_id_type=MESH)
        return carry

    lax.fori_loop(1, devices, greet, 0)
    gain = gain_ref[...]
    for t in range(tok):
        slab_f32[t * width : (t + 1) * width, :] = normalize(slab_ref[t].astype(F32), gain)

    def chunk(p):
        parts = [
            slab_f32[pl.ds(p * cols + jj, tok, stride=width), :] for jj in range(cols)
        ]
        return jnp.concatenate(parts, axis=0).astype(BF16)

    slab_recv[me] = chunk(me)
    pl.semaphore_wait(barrier, devices - 1)

    def slab_copy(p):
        return pltpu.make_async_remote_copy(
            src_ref=slab_send.at[p],
            dst_ref=slab_recv.at[me],
            send_sem=slab_ss.at[p],
            recv_sem=slab_rs.at[me],
            device_id=place(p),
            device_id_type=MESH,
        )

    def send_slab(n, carry):
        p = lax.rem(me + n, devices)
        slab_send[p] = chunk(p)
        slab_copy(p).start()
        return carry

    lax.fori_loop(1, devices, send_slab, 0)

    pair_f32[...] = pair_ref[...].astype(F32).reshape(key_blk * query_blk, channels)
    lane_head = lax.broadcasted_iota(jnp.int32, (heads, lanes), 1) // query_blk
    spread_mat = (lane_head == lax.broadcasted_iota(jnp.int32, (heads, lanes), 0)).astype(F32)
    wide = jnp.dot(wb_ref[...], spread_mat.astype(BF16), preferred_element_type=F32)
    lane_query = lax.rem(lax.broadcasted_iota(jnp.int32, (channels, lanes), 1), query_blk)

    def bias_step(il, total):
        rows = pair_f32[pl.ds(il, key_blk, stride=query_blk), :]
        normed = normalize(rows, gain).astype(BF16)
        weight = jnp.where(lane_query == il, wide, 0.0).astype(BF16)
        return total + jnp.dot(normed, weight, preferred_element_type=F32)

    total = lax.fori_loop(
        0, query_blk, bias_step, jnp.zeros((key_blk, lanes), F32), unroll=8
    )
    bias[my_col, my_row] = total.astype(BF16)

    def bias_copy(p):
        return pltpu.make_async_remote_copy(
            src_ref=bias.at[my_col, my_row],
            dst_ref=bias.at[my_col, my_row],
            send_sem=bias_ss.at[p],
            recv_sem=bias_rs.at[me],
            device_id=place(p),
            device_id_type=MESH,
        )

    def relay_copy(s):
        r, c = place(s)
        return pltpu.make_async_remote_copy(
            src_ref=bias.at[c, r],
            dst_ref=bias.at[c, r],
            send_sem=relay_ss.at[s],
            recv_sem=bias_rs.at[s],
            device_id=place(sibling),
            device_id_type=MESH,
        )

    def bias_wait(s):
        r, c = place(s)
        pltpu.make_async_remote_copy(
            src_ref=bias.at[c, r],
            dst_ref=bias.at[c, r],
            send_sem=relay_ss.at[s],
            recv_sem=bias_rs.at[s],
            device_id=place(sibling),
            device_id_type=MESH,
        ).wait_recv()

    bias_copy(sibling).start()

    def send_bias(n, carry):
        bias_copy(lax.rem(me + cores * n, devices)).start()
        return carry

    lax.fori_loop(1, devices // cores, send_bias, 0)

    def take_slab(n, carry):
        s = lax.rem(me + devices - n, devices)
        pltpu.make_async_remote_copy(
            src_ref=slab_send.at[s],
            dst_ref=slab_recv.at[s],
            send_sem=slab_ss.at[s],
            recv_sem=slab_rs.at[s],
            device_id=place(s),
            device_id_type=MESH,
        ).wait_recv()
        return carry

    lax.fori_loop(1, devices, take_slab, 0)
    chunk_f32[...] = slab_recv[...].astype(F32)
    value_w = wv_ref[...].astype(F32).T.astype(BF16)
    for jj in range(cols):
        rows = chunk_f32[:, jj * tok : (jj + 1) * tok, :].reshape(tokens, channels).astype(BF16)
        query[jj] = jnp.dot(rows, wq_ref[...], preferred_element_type=F32).astype(BF16)
        key[jj] = jnp.dot(rows, wk_ref[...], preferred_element_type=F32).astype(BF16)
        value_t[jj] = lax.dot_general(
            value_w, rows, NT, preferred_element_type=F32
        ).astype(BF16)
        gate[jj] = jax.nn.sigmoid(
            jnp.dot(rows, wg_ref[...], preferred_element_type=F32) + gate_bias_ref[...]
        )
    shift_row = (mask_ref[...].astype(F32) - 1.0) * 1000000000.0
    shift[...] = jnp.broadcast_to(shift_row, (lanes, tokens)).T

    def relay(n, carry):
        s = lax.rem(me + devices - cores * n, devices)
        bias_wait(s)
        relay_copy(s).start()
        return carry

    lax.fori_loop(1, devices // cores, relay, 0)

    row_head = lax.broadcasted_iota(jnp.int32, (lanes, channels), 0) // query_blk
    chan_head = lax.broadcasted_iota(jnp.int32, (lanes, channels), 1) // head_dim
    own_head = row_head == chan_head

    def back_copy(p):
        return pltpu.make_async_remote_copy(
            src_ref=back_send.at[p],
            dst_ref=back_recv.at[me],
            send_sem=back_ss.at[p],
            recv_sem=back_rs.at[me],
            device_id=place(p),
            device_id_type=MESH,
        )

    def attend(n, carry):
        c = lax.rem(my_col + n, cols_count)
        for r in range(rows_count):
            s = r * cols_count + c

            @pl.when(lax.rem(c + my_col, 2) == 1)
            def _():
                bias_wait(s)

        bias_f32 = bias[c].astype(F32).reshape(tokens, lanes)
        at = pl.multiple_of(c * query_blk, query_blk)
        hidden = []
        for jj in range(cols):
            q_rows = query[jj, pl.ds(at, query_blk), :].astype(F32)
            q_heads = jnp.where(
                own_head, jnp.concatenate([q_rows] * heads, axis=0), 0.0
            ).astype(BF16)
            scores = lax.dot_general(key[jj], q_heads, NT, preferred_element_type=F32) * scale
            scores = (scores + bias_f32) + shift[...]
            top = jnp.max(scores, axis=0, keepdims=True)
            weights = jnp.exp(scores - top)
            denom = jnp.sum(weights, axis=0, keepdims=True)
            numer = jnp.dot(value_t[jj], weights.astype(BF16), preferred_element_type=F32)
            spread = jnp.where(own_head, (numer * (1.0 / denom)).T, 0.0)
            attended = spread[:query_blk]
            for h in range(1, heads):
                attended = attended + spread[h * query_blk : (h + 1) * query_blk]
            hidden.append((gate[jj, pl.ds(at, query_blk), :] * attended).astype(BF16))
        update = (
            jnp.dot(jnp.concatenate(hidden, axis=0), wo_ref[...], preferred_element_type=F32)
            + out_bias_ref[...]
        )
        for o in range(owners):
            p = c * owners + o
            part = jnp.concatenate(
                [
                    update[jj * query_blk + o * tok : jj * query_blk + (o + 1) * tok]
                    for jj in range(cols)
                ],
                axis=0,
            ).astype(BF16)

            @pl.when(p == me)
            def _():
                back_recv[me] = part

            @pl.when(p != me)
            def _():
                back_send[p] = part
                back_copy(p).start()

        return carry

    lax.fori_loop(0, cols_count, attend, 0)

    def take_back(n, carry):
        s = lax.rem(me + devices - n, devices)
        pltpu.make_async_remote_copy(
            src_ref=back_send.at[s],
            dst_ref=back_recv.at[s],
            send_sem=back_ss.at[s],
            recv_sem=back_rs.at[s],
            device_id=place(s),
            device_id_type=MESH,
        ).wait_recv()
        return carry

    lax.fori_loop(1, devices, take_back, 0)
    slab_f32[...] = back_recv[...].astype(F32).reshape(width * tok, channels)
    for t in range(tok):
        out_ref[t] = slab_f32[pl.ds(t, width, stride=tok), :].astype(BF16)

    def drain(n, carry):
        p = lax.rem(me + n, devices)
        slab_copy(p).wait_send()
        back_copy(p).wait_send()
        return carry

    lax.fori_loop(1, devices, drain, 0)
    bias_copy(sibling).wait_send()

    def drain_bias(n, carry):
        bias_copy(lax.rem(me + cores * n, devices)).wait_send()
        relay_copy(lax.rem(me + devices - cores * n, devices)).wait_send()
        return carry

    lax.fori_loop(1, devices // cores, drain_bias, 0)


def per_device(
    slab, pair, mask, ln_gain, w_query, w_key, w_value, w_gate, gate_bias, w_bias, w_out, out_bias
):
    rows_count = lax.axis_size("row")
    cols_count = lax.axis_size("col")
    devices = rows_count * cols_count
    tok, width, channels = slab.shape
    key_blk, query_blk, _ = pair.shape
    heads = w_bias.shape[1]
    cols = width // devices
    tokens = devices * tok
    lanes = heads * query_blk
    dma = pltpu.SemaphoreType.DMA((devices,))
    vmem = pltpu.VMEM
    return pl.pallas_call(
        functools.partial(kernel, rows_count, cols_count),
        out_shape=jax.ShapeDtypeStruct(slab.shape, BF16),
        in_specs=[pl.BlockSpec(memory_space=vmem)] * 12,
        out_specs=pl.BlockSpec(memory_space=vmem),
        scratch_shapes=[
            vmem((tok * width, channels), F32),
            vmem((key_blk * query_blk, channels), F32),
            vmem((devices, cols * tok, channels), BF16),
            vmem((devices, cols * tok, channels), BF16),
            vmem((cols_count, rows_count, key_blk, lanes), BF16),
            vmem((devices, cols * tok, channels), F32),
            vmem((cols, tokens, channels), BF16),
            vmem((cols, tokens, channels), BF16),
            vmem((cols, channels, tokens), BF16),
            vmem((cols, tokens, channels), F32),
            vmem((tokens, lanes), F32),
            vmem((devices, cols * tok, channels), BF16),
            vmem((devices, cols * tok, channels), BF16),
            dma,
            dma,
            dma,
            dma,
            dma,
            dma,
            dma,
        ],
        compiler_params=pltpu.CompilerParams(
            collective_id=0, has_side_effects=True, vmem_limit_bytes=48 * 1024 * 1024
        ),
        cost_estimate=pl.CostEstimate(
            flops=2 * tokens * tokens * heads * channels * cols * 2,
            bytes_accessed=4 * slab.size,
            transcendentals=tokens * tokens * heads * cols,
        ),
        name="triangle",
    )(
        slab,
        pair,
        mask.reshape(1, -1),
        ln_gain.reshape(1, -1),
        w_query,
        w_key,
        w_value,
        w_gate,
        gate_bias.reshape(1, -1),
        w_bias,
        w_out,
        out_bias.reshape(1, -1),
    )


def solution(mesh):
    placed = (P(("row", "col"), None, None), P("row", "col", None)) + (P(),) * 10
    return jax.shard_map(
        per_device,
        mesh=mesh,
        in_specs=placed,
        out_specs=P(("row", "col"), None, None),
        check_vma=False,
    )
```

time: 251 us -> 39.8 us (0.16)
  waiting for transfers between devices: 143 us -> 0 us
  Pallas kernels: 0 us -> 32.6 us
  matrix products: 25.3 us -> 0 us
  other arithmetic: 22.8 us -> 0 us
  local copies, waits for them, and re-layouts: 28.9 us -> 6.61 us
  between operations: 14.1 us -> 0.06 us
  blocking collectives: 11.8 us -> 0 us
  starting transfers between devices: 4.09 us -> 0 us
    pmax x1 -> x0, waiting for transfers between devices: 46.7 us -> none  [per_device(): lax.pmax(local_top.astype(jnp.bfloat16), 'col').astype(local_top.dtype)]
    unnamed x6 -> x0, waiting for transfers between devices: 40.2 us -> none
    reduce_scatter x1 -> x0, waiting for transfers between devices: 36.1 us -> none  [per_device(): lax.psum_scatter(numer.astype(jnp.bfloat16), 'col', scatter_dimension=0,...]
    pallas_call x0 -> x1, Pallas kernels: none -> 32.6 us  [per_device(): pl.pallas_call(functools.partial(kernel, rows_count, cols_count), out_sha...]
    dot_general x6 -> x0, matrix products: 25.3 us -> none  [the longest x1 8.53 us: one_block(): jnp.einsum('ijhd,kjhd->ihjk', query_blk, keys_split, preferred_element_ty...]
    all_gather x2 -> x0, waiting for transfers between devices: 16.4 us -> none  [the longest x1 13.1 us: per_device(): lax.all_gather(slab, 'col', axis=0, tiled=True)]
    reduce_sum x8 -> x0, other arithmetic: 13.4 us -> none  [the longest x4 7.95 us: normalize(): spread = jnp.mean(jnp.square(values - center), axis=-1, keepdims=True)]
    all_to_all x1 -> x0, blocking collectives: 11.8 us -> none  [per_device(): lax.all_to_all(bias_tile, 'col', split_axis=1, concat_axis=2, tiled=True)]
  transfers between devices with their start and end apart: 6 -> 0, of which waited for: 6 -> 0; matrix products, arithmetic and copies ran while one was open for 19% -> 0% of each run, Pallas kernels for 0% -> 0%
where the time goes in v1:
time: 39.8 us; the launch traced here: 39.3 us
  Pallas kernels  32.6 us (82%)
  local copies, waits for them, and re-layouts  6.61 us (17%)
    pallas_call x1, Pallas kernels, per_device(): pl.pallas_call(functools.partial(kernel, rows_count, cols_count), out_sha...  32.6 us
    unnamed x24, local copies, waits for them, and re-layouts  6.61 us

profile of v1, /device:TPU:0, one launch (start us, length us, event | category | flops | bytes accessed | tf_op | source)
XLA Modules:
  0.0 39.3 jit_solution(84686694737110095)
XLA Ops:
  0.0 0.0 copy-start.2
  0.0 0.0 copy-start.7
  0.0 0.0 copy-start.8
  0.0 0.0 copy-start.9
  0.0 0.0 copy-start.10
  0.0 0.9 %copy.13.wb_ref = bf16[128,4]{1,0:T(8,128)(2,1)S(1)} copy(bf16[128,4]{0,1:T(4,128)(2,1)} %param.21) | data formatting | bytes 2048 | tf_op args[9]
  0.9 0.0 copy-done.2
  0.9 0.0 copy-done.7
  0.9 0.0 copy-done.8
  0.9 0.0 copy-done.9
  0.9 0.0 copy-done.10
  0.9 0.0 copy-start
  0.9 1.0 %copy-done = bf16[64,32,128]{2,1,0:T(8,128)(2,1)S(1)} copy-done((bf16[64,32,128]{2,1,0:T(8,128)(2,1)S(1)}, bf16[64,32,128]{2,1,0:T(8,128)(2,1)}, u32[]{:S(2)}) %copy-start) | copy-done | bytes 524312
  2.0 0.0 copy-start.1
  2.0 0.9 %copy-done.1 = bf16[8,128,128]{2,1,0:T(8,128)(2,1)S(1)} copy-done((bf16[8,128,128]{2,1,0:T(8,128)(2,1)S(1)}, bf16[8,128,128]{2,1,0:T(8,128)(2,1)}, u32[]{:S(2)}) %copy-start.1) | copy-done | bytes 262168
  2.9 0.0 copy-start.3
  2.9 0.8 %copy-done.3 = bf16[128,128]{1,0:T(8,128)(2,1)S(1)} copy-done((bf16[128,128]{1,0:T(8,128)(2,1)S(1)}, bf16[128,128]{1,0:T(8,128)(2,1)}, u32[]{:S(2)}) %copy-start.3) | copy-done | bytes 32792
  3.7 0.0 copy-start.4
  3.7 0.8 %copy-done.4 = bf16[128,128]{1,0:T(8,128)(2,1)S(1)} copy-done((bf16[128,128]{1,0:T(8,128)(2,1)S(1)}, bf16[128,128]{1,0:T(8,128)(2,1)}, u32[]{:S(2)}) %copy-start.4) | copy-done | bytes 32792
  4.4 0.0 copy-start.5
  4.4 0.8 %copy-done.5 = bf16[128,128]{1,0:T(8,128)(2,1)S(1)} copy-done((bf16[128,128]{1,0:T(8,128)(2,1)S(1)}, bf16[128,128]{1,0:T(8,128)(2,1)}, u32[]{:S(2)}) %copy-start.5) | copy-done | bytes 32792
  5.2 0.0 copy-start.6
  5.2 0.8 %copy-done.6 = bf16[128,128]{1,0:T(8,128)(2,1)S(1)} copy-done((bf16[128,128]{1,0:T(8,128)(2,1)S(1)}, bf16[128,128]{1,0:T(8,128)(2,1)}, u32[]{:S(2)}) %copy-start.6) | copy-done | bytes 32792
  6.0 32.6 %triangle.1 = bf16[8,128,128]{2,1,0:T(8,128)(2,1)S(1)} custom-call(bf16[8,128,128]{2,1,0:T(8,128)(2,1)S(1)} %copy-done.1, bf16[64,32,128]{2,1,0:T(8,128)(2,1)S(1)} %copy-done, s32[1,256]{1,0:T(1,128)S(1)} %bitcast.4, f32[1,128]{1,0:T(1,128)S(1)} %bitcast.5, bf16[128,128]{1,0:T(8,128)(2,1)S(1)} %copy-done.2, bf16[128,128]{1,0:T(8,128)(2,1)S(1)} %copy-done.3, ...), custom_call_target="tpu_custom_call" | custom-call | flops 536870912 | bytes 524288 | tf_op jit(solution)/shard_map/triangle/pallas_call | solution.py:328
  38.6 0.7 %copy.15 = bf16[8,128,128]{2,1,0:T(8,128)(2,1)} copy(bf16[8,128,128]{2,1,0:T(8,128)(2,1)S(1)} %triangle.1) | data formatting | bytes 524288
Async XLA Ops:
  0.0 0.9 %copy-start.2 = (bf16[128,128]{1,0:T(8,128)(2,1)S(1)}, bf16[128,128]{1,0:T(8,128)(2,1)}, u32[]{:S(2)}) copy-start(bf16[128,128]{1,0:T(8,128)(2,1)} %wq_ref.1) | copy-start | bytes 98308
  0.0 0.9 %copy-start.7 = (s32[256]{0:T(256)S(1)}, s32[256]{0:T(256)}, u32[]{:S(2)}) copy-start(s32[256]{0:T(256)} %param.14) | copy-start | bytes 3076
  0.0 0.9 %copy-start.8 = (f32[128]{0:T(128)S(1)}, f32[128]{0:T(128)}, u32[]{:S(2)}) copy-start(f32[128]{0:T(128)} %param.15) | copy-start | bytes 1540
  0.0 0.9 %copy-start.9 = (f32[128]{0:T(128)S(1)}, f32[128]{0:T(128)}, u32[]{:S(2)}) copy-start(f32[128]{0:T(128)} %param.20) | copy-start | bytes 1540
  0.0 0.9 %copy-start.10 = (f32[128]{0:T(128)S(1)}, f32[128]{0:T(128)}, u32[]{:S(2)}) copy-start(f32[128]{0:T(128)} %param.23) | copy-start | bytes 1540
  0.9 1.0 %copy-start = (bf16[64,32,128]{2,1,0:T(8,128)(2,1)S(1)}, bf16[64,32,128]{2,1,0:T(8,128)(2,1)}, u32[]{:S(2)}) copy-start(bf16[64,32,128]{2,1,0:T(8,128)(2,1)} %pair_ref.1) | copy-start | bytes 1572868
  2.0 0.9 %copy-start.1 = (bf16[8,128,128]{2,1,0:T(8,128)(2,1)S(1)}, bf16[8,128,128]{2,1,0:T(8,128)(2,1)}, u32[]{:S(2)}) copy-start(bf16[8,128,128]{2,1,0:T(8,128)(2,1)} %slab_ref.1) | copy-start | bytes 786436
  2.9 0.8 %copy-start.3 = (bf16[128,128]{1,0:T(8,128)(2,1)S(1)}, bf16[128,128]{1,0:T(8,128)(2,1)}, u32[]{:S(2)}) copy-start(bf16[128,128]{1,0:T(8,128)(2,1)} %wk_ref.1) | copy-start | bytes 98308
  3.7 0.8 %copy-start.4 = (bf16[128,128]{1,0:T(8,128)(2,1)S(1)}, bf16[128,128]{1,0:T(8,128)(2,1)}, u32[]{:S(2)}) copy-start(bf16[128,128]{1,0:T(8,128)(2,1)} %wv_ref.1) | copy-start | bytes 98308
  4.4 0.8 %copy-start.5 = (bf16[128,128]{1,0:T(8,128)(2,1)S(1)}, bf16[128,128]{1,0:T(8,128)(2,1)}, u32[]{:S(2)}) copy-start(bf16[128,128]{1,0:T(8,128)(2,1)} %wg_ref.1) | copy-start | bytes 98308
  5.2 0.8 %copy-start.6 = (bf16[128,128]{1,0:T(8,128)(2,1)S(1)}, bf16[128,128]{1,0:T(8,128)(2,1)}, u32[]{:S(2)}) copy-start(bf16[128,128]{1,0:T(8,128)(2,1)} %wo_ref.1) | copy-start | bytes 98308

commit v2 on v1

v2 whole, which is shorter than its diff:
```python
import functools
import math

import jax
import jax.numpy as jnp
from jax import lax
from jax.experimental import pallas as pl
from jax.experimental.pallas import tpu as pltpu
from jax.sharding import PartitionSpec as P

MESH = pl.DeviceIdType.MESH
F32 = jnp.float32
BF16 = jnp.bfloat16
NT = (((1,), (1,)), ((), ()))


def normalize(values, gain):
    center = jnp.mean(values, axis=-1, keepdims=True)
    moved = values - center
    spread = jnp.mean(jnp.square(moved), axis=-1, keepdims=True)
    return moved * lax.rsqrt(spread + 1e-05) * gain


def kernel(rows_count, cols_count, *refs):
    hbm, out_ref = refs[:12], refs[12]
    (
        slab_ref,
        pair_ref,
        mask_ref,
        gain_ref,
        wq_ref,
        wk_ref,
        wv_ref,
        wg_ref,
        gate_bias_ref,
        wb_ref,
        wo_ref,
        out_bias_ref,
    ) = local = refs[13:25]
    (
        slab_f32,
        pair_f32,
        slab_send,
        slab_recv,
        bias,
        chunk_f32,
        query,
        key,
        value_t,
        gate,
        shift,
        back_send,
        back_recv,
        in_sem,
        slab_ss,
        slab_rs,
        line_ss,
        line_rs,
        plane_ss,
        plane_rs,
        core_ss,
        core_rs,
        back_ss,
        back_rs,
    ) = refs[25:]
    devices = rows_count * cols_count
    tok, width, channels = slab_ref.shape
    key_blk, query_blk, _ = pair_ref.shape
    heads = wb_ref.shape[0]
    head_dim = channels // heads
    cols = width // devices
    tokens = devices * tok
    lanes = heads * query_blk
    owners = query_blk // tok
    scale = 1.0 / math.sqrt(head_dim)
    cores = 2
    line = cols_count // cores
    my_row, my_col = lax.axis_index("row"), lax.axis_index("col")
    my_line, core = lax.div(my_col, cores), lax.rem(my_col, cores)
    me = my_row * cols_count + my_col

    def fetch(i):
        return pltpu.make_async_copy(hbm[i], local[i], in_sem.at[i])

    for i in (0, 3, 1, 9, 2, 4, 5, 6, 7, 8, 10, 11):
        fetch(i).start()

    def place(p):
        return (lax.div(p, cols_count), lax.rem(p, cols_count))

    def wait_bytes(ref, sem):
        pltpu.make_async_copy(ref, ref, sem).wait()

    def send(src, dst, send_sem, recv_sem, target):
        pltpu.make_async_remote_copy(
            src_ref=src,
            dst_ref=dst,
            send_sem=send_sem,
            recv_sem=recv_sem,
            device_id=target,
            device_id_type=MESH,
        ).start()

    barrier = pltpu.get_barrier_semaphore()

    def greet(n, carry):
        p = lax.rem(me + n, devices)
        pl.semaphore_signal(barrier, inc=1, device_id=place(p), device_id_type=MESH)
        return carry

    lax.fori_loop(1, devices, greet, 0)

    fetch(0).wait()
    fetch(3).wait()
    gain = gain_ref[...]
    for t in range(tok):
        slab_f32[t * width : (t + 1) * width, :] = normalize(slab_ref[t].astype(F32), gain)
    for p in range(devices):
        parts = [
            slab_f32[pl.ds(p * cols + jj, tok, stride=width), :] for jj in range(cols)
        ]
        slab_send[p] = jnp.concatenate(parts, axis=0).astype(BF16)
    slab_recv[me] = slab_send[me]
    pl.semaphore_wait(barrier, devices - 1)

    def send_slab(n, carry):
        p = lax.rem(me + n, devices)
        send(slab_send.at[p], slab_recv.at[me], slab_ss, slab_rs, place(p))
        return carry

    lax.fori_loop(1, devices, send_slab, 0)

    fetch(1).wait()
    fetch(9).wait()
    pair_f32[...] = pair_ref[...].astype(F32).reshape(key_blk * query_blk, channels)
    lane_head = lax.broadcasted_iota(jnp.int32, (heads, lanes), 1) // query_blk
    spread_mat = (lane_head == lax.broadcasted_iota(jnp.int32, (heads, lanes), 0)).astype(F32)
    wide = lax.dot_general(
        wb_ref[...],
        spread_mat.astype(BF16),
        (((0,), (0,)), ((), ())),
        preferred_element_type=F32,
    )
    lane_query = lax.rem(lax.broadcasted_iota(jnp.int32, (channels, lanes), 1), query_blk)

    def bias_step(il, total):
        rows = pair_f32[pl.ds(il, key_blk, stride=query_blk), :]
        normed = normalize(rows, gain).astype(BF16)
        weight = jnp.where(lane_query == il, wide, 0.0).astype(BF16)
        return total + jnp.dot(normed, weight, preferred_element_type=F32)

    total = lax.fori_loop(
        0, query_blk, bias_step, jnp.zeros((key_blk, lanes), F32), unroll=8
    )
    bias[core, my_row, my_line] = total.astype(BF16)
    for n in range(1, line):
        z = lax.rem(my_line + n, line)
        tile = bias.at[core, my_row, my_line]
        send(tile, tile, line_ss, line_rs, (my_row, z * cores + core))

    wait_bytes(slab_recv.at[pl.ds(0, devices - 1)], slab_rs)
    chunk_f32[...] = slab_recv[...].astype(F32)

    wait_bytes(bias.at[core, my_row, pl.ds(0, line - 1)], line_rs)
    block = bias.at[core, my_row]
    for n in range(1, rows_count):
        r = lax.rem(my_row + n, rows_count)
        send(block, block, plane_ss, plane_rs, (r, my_col))
    send(block, block, core_ss, core_rs, (my_row, my_col + 1 - 2 * core))

    for i in (2, 4, 5, 6, 7, 8, 10, 11):
        fetch(i).wait()
    value_w = wv_ref[...].astype(F32).T.astype(BF16)
    for jj in range(cols):
        rows = chunk_f32[:, jj * tok : (jj + 1) * tok, :].reshape(tokens, channels).astype(BF16)
        query[jj] = jnp.dot(rows, wq_ref[...], preferred_element_type=F32).astype(BF16)
        key[jj] = jnp.dot(rows, wk_ref[...], preferred_element_type=F32).astype(BF16)
        value_t[jj] = lax.dot_general(
            value_w, rows, NT, preferred_element_type=F32
        ).astype(BF16)
        gate[jj] = jax.nn.sigmoid(
            jnp.dot(rows, wg_ref[...], preferred_element_type=F32) + gate_bias_ref[...]
        )
    shift_row = (mask_ref[...].astype(F32) - 1.0) * 1000000000.0
    shift[...] = jnp.broadcast_to(shift_row, (lanes, tokens)).T

    wait_bytes(bias.at[core, pl.ds(0, rows_count - 1)], plane_rs)
    for n in range(1, rows_count):
        other = bias.at[core, lax.rem(my_row + n, rows_count)]
        send(other, other, core_ss, core_rs, (my_row, my_col + 1 - 2 * core))

    row_head = lax.broadcasted_iota(jnp.int32, (lanes, channels), 0) // query_blk
    chan_head = lax.broadcasted_iota(jnp.int32, (lanes, channels), 1) // head_dim
    own_head = row_head == chan_head

    def attend_block(half, z):
        c = z * cores + half
        bias_f32 = bias[half, :, z].astype(F32).reshape(tokens, lanes)
        at = pl.multiple_of(c * query_blk, query_blk)
        hidden = []
        for jj in range(cols):
            q_rows = query[jj, pl.ds(at, query_blk), :].astype(F32)
            q_heads = jnp.where(
                own_head, jnp.concatenate([q_rows] * heads, axis=0), 0.0
            ).astype(BF16)
            scores = lax.dot_general(key[jj], q_heads, NT, preferred_element_type=F32) * scale
            scores = (scores + bias_f32) + shift[...]
            top = jnp.max(scores, axis=0, keepdims=True)
            weights = jnp.exp(scores - top)
            denom = jnp.sum(weights, axis=0, keepdims=True)
            numer = jnp.dot(value_t[jj], weights.astype(BF16), preferred_element_type=F32)
            spread = jnp.where(own_head, (numer * (1.0 / denom)).T, 0.0)
            attended = spread[:query_blk]
            for h in range(1, heads):
                attended = attended + spread[h * query_blk : (h + 1) * query_blk]
            hidden.append((gate[jj, pl.ds(at, query_blk), :] * attended).astype(BF16))
        update = (
            jnp.dot(jnp.concatenate(hidden, axis=0), wo_ref[...], preferred_element_type=F32)
            + out_bias_ref[...]
        )
        for o in range(owners):
            back_send[c * owners + o] = jnp.concatenate(
                [
                    update[jj * query_blk + o * tok : jj * query_blk + (o + 1) * tok]
                    for jj in range(cols)
                ],
                axis=0,
            ).astype(BF16)

    def send_back(half, z):
        for o in range(owners):
            p = (z * cores + half) * owners + o

            @pl.when(p != me)
            def _():
                send(back_send.at[p], back_recv.at[me], back_ss, back_rs, place(p))

    pair_step = 2 if line % 2 == 0 else 1

    def attend_half(half):
        def step(n, carry):
            first = lax.rem(lax.div(my_line, pair_step) + n, line // pair_step) * pair_step
            for m in range(pair_step):
                attend_block(half, first + m)
            for m in range(pair_step):
                send_back(half, first + m)
            return carry

        lax.fori_loop(0, line // pair_step, step, 0)

    attend_half(core)
    wait_bytes(bias.at[1 - core], core_rs)
    attend_half(1 - core)
    back_recv[me] = back_send[me]

    wait_bytes(slab_send.at[pl.ds(0, devices - 1)], slab_ss)
    wait_bytes(bias.at[core, my_row, pl.ds(0, line - 1)], line_ss)
    wait_bytes(bias.at[core, pl.ds(0, rows_count - 1)], plane_ss)
    wait_bytes(bias.at[core], core_ss)
    wait_bytes(back_send.at[pl.ds(0, devices - 1)], back_ss)

    wait_bytes(back_recv.at[pl.ds(0, devices - 1)], back_rs)
    slab_f32[...] = back_recv[...].astype(F32).reshape(width * tok, channels)
    for t in range(tok):
        out_ref[t] = slab_f32[pl.ds(t, width, stride=tok), :].astype(BF16)


def per_device(
    slab, pair, mask, ln_gain, w_query, w_key, w_value, w_gate, gate_bias, w_bias, w_out, out_bias
):
    rows_count = lax.axis_size("row")
    cols_count = lax.axis_size("col")
    devices = rows_count * cols_count
    tok, width, channels = slab.shape
    key_blk, query_blk, _ = pair.shape
    heads = w_bias.shape[1]
    cols = width // devices
    tokens = devices * tok
    lanes = heads * query_blk
    operands = (
        slab,
        pair,
        mask.reshape(1, -1),
        ln_gain.reshape(1, -1),
        w_query,
        w_key,
        w_value,
        w_gate,
        gate_bias.reshape(1, -1),
        w_bias.T,
        w_out,
        out_bias.reshape(1, -1),
    )
    dma = pltpu.SemaphoreType.DMA
    vmem = pltpu.VMEM
    return pl.pallas_call(
        functools.partial(kernel, rows_count, cols_count),
        out_shape=jax.ShapeDtypeStruct(slab.shape, BF16),
        in_specs=[pl.BlockSpec(memory_space=pltpu.HBM)] * len(operands),
        out_specs=pl.BlockSpec(memory_space=vmem),
        scratch_shapes=[vmem(x.shape, x.dtype) for x in operands]
        + [
            vmem((tok * width, channels), F32),
            vmem((key_blk * query_blk, channels), F32),
            vmem((devices, cols * tok, channels), BF16),
            vmem((devices, cols * tok, channels), BF16),
            vmem((2, rows_count, cols_count // 2, key_blk, lanes), BF16),
            vmem((devices, cols * tok, channels), F32),
            vmem((cols, tokens, channels), BF16),
            vmem((cols, tokens, channels), BF16),
            vmem((cols, channels, tokens), BF16),
            vmem((cols, tokens, channels), F32),
            vmem((tokens, lanes), F32),
            vmem((devices, cols * tok, channels), BF16),
            vmem((devices, cols * tok, channels), BF16),
            dma((len(operands),)),
        ]
        + [dma] * 10,
        compiler_params=pltpu.CompilerParams(
            collective_id=0, has_side_effects=True, vmem_limit_bytes=56 * 1024 * 1024
        ),
        cost_estimate=pl.CostEstimate(
            flops=2 * tokens * tokens * heads * channels * cols * 2,
            bytes_accessed=4 * slab.size,
            transcendentals=tokens * tokens * heads * cols,
        ),
        name="triangle",
    )(*operands)


def solution(mesh):
    placed = (P(("row", "col"), None, None), P("row", "col", None)) + (P(),) * 10
    return jax.shard_map(
        per_device,
        mesh=mesh,
        in_specs=placed,
        out_specs=P(("row", "col"), None, None),
        check_vma=False,
    )
```

time: 39.8 us -> 33.6 us (0.84)
  local copies, waits for them, and re-layouts: 6.61 us -> 1.67 us
  Pallas kernels: 32.6 us -> 31.8 us
    unnamed x24 -> x1, local copies, waits for them, and re-layouts: 6.61 us -> 1.67 us
    pallas_call x1, Pallas kernels: 32.6 us -> 31.8 us  [per_device(): pl.pallas_call(functools.partial(kernel, rows_count, cols_count), out_sha...]
where the time goes in v2:
time: 33.6 us; the launch traced here: 33.4 us
  Pallas kernels  31.8 us (95%)
  local copies, waits for them, and re-layouts  1.67 us (5%)
    pallas_call x1, Pallas kernels, per_device(): pl.pallas_call(functools.partial(kernel, rows_count, cols_count), out_sha...  31.8 us
    unnamed x1, local copies, waits for them, and re-layouts  1.67 us

profile of v2, /device:TPU:0, one launch (start us, length us, event | category | flops | bytes accessed | tf_op | source)
XLA Modules:
  0.0 33.4 jit_solution(9888587916848849153)
XLA Ops:
  0.0 31.8 %triangle.1 = bf16[8,128,128]{2,1,0:T(8,128)(2,1)} custom-call(bf16[8,128,128]{2,1,0:T(8,128)(2,1)} %refs_0_.1, bf16[64,32,128]{2,1,0:T(8,128)(2,1)} %refs_1_.1, s32[1,256]{1,0:T(1,128)} %bitcast.5, f32[1,128]{1,0:T(1,128)} %bitcast.7, bf16[128,128]{1,0:T(8,128)(2,1)} %refs_4_.1, bf16[128,128]{1,0:T(8,128)(2,1)} %refs_5_.1, bf16[128,128]{1,0:T(8,128)(2,1)} %refs_6_.1, ...), custom_call_target="tpu_custom_call" | custom-call | flops 536870912 | bytes 524288 | tf_op jit(solution)/shard_map/triangle/pallas_call | solution.py:296
  31.8 1.7 %copy.14 = bf16[8,128,128]{2,1,0:T(8,128)(2,1)} copy(bf16[8,128,128]{2,1,0:T(8,128)(2,1)} %triangle.1) | data formatting | bytes 524288

commit v3 on v2

--- a/solution.py
+++ b/solution.py
@@ -39,7 +39,6 @@
     ) = local = refs[13:25]
     (
         slab_f32,
-        pair_f32,
         slab_send,
         slab_recv,
         bias,
@@ -75,6 +74,7 @@
     scale = 1.0 / math.sqrt(head_dim)
     cores = 2
     line = cols_count // cores
+    group = 2 - line % 2
     my_row, my_col = lax.axis_index("row"), lax.axis_index("col")
     my_line, core = lax.div(my_col, cores), lax.rem(my_col, cores)
     me = my_row * cols_count + my_col
@@ -132,7 +132,6 @@
 
     fetch(1).wait()
     fetch(9).wait()
-    pair_f32[...] = pair_ref[...].astype(F32).reshape(key_blk * query_blk, channels)
     lane_head = lax.broadcasted_iota(jnp.int32, (heads, lanes), 1) // query_blk
     spread_mat = (lane_head == lax.broadcasted_iota(jnp.int32, (heads, lanes), 0)).astype(F32)
     wide = lax.dot_general(
@@ -140,19 +139,16 @@
         spread_mat.astype(BF16),
         (((0,), (0,)), ((), ())),
         preferred_element_type=F32,
-    )
-    lane_query = lax.rem(lax.broadcasted_iota(jnp.int32, (channels, lanes), 1), query_blk)
-
-    def bias_step(il, total):
-        rows = pair_f32[pl.ds(il, key_blk, stride=query_blk), :]
+    ).astype(BF16)
+    part = 16
+    lane_query = lax.rem(lax.broadcasted_iota(jnp.int32, (part, query_blk, lanes), 2), query_blk)
+    own_query = lane_query == lax.broadcasted_iota(jnp.int32, (part, query_blk, lanes), 1)
+    for k in range(0, key_blk, part):
+        rows = pair_ref[k : k + part].astype(F32).reshape(part * query_blk, channels)
         normed = normalize(rows, gain).astype(BF16)
-        weight = jnp.where(lane_query == il, wide, 0.0).astype(BF16)
-        return total + jnp.dot(normed, weight, preferred_element_type=F32)
-
-    total = lax.fori_loop(
-        0, query_blk, bias_step, jnp.zeros((key_blk, lanes), F32), unroll=8
-    )
-    bias[core, my_row, my_line] = total.astype(BF16)
+        spread = jnp.dot(normed, wide, preferred_element_type=F32)
+        spread = jnp.where(own_query, spread.reshape(part, query_blk, lanes), 0.0)
+        bias[core, my_row, my_line, k : k + part, :] = jnp.sum(spread, axis=1).astype(BF16)
     for n in range(1, line):
         z = lax.rem(my_line + n, line)
         tile = bias.at[core, my_row, my_line]
@@ -170,39 +166,42 @@
 
     for i in (2, 4, 5, 6, 7, 8, 10, 11):
         fetch(i).wait()
+    weights_qkg = jnp.concatenate([wq_ref[...], wk_ref[...], wg_ref[...]], axis=1)
     value_w = wv_ref[...].astype(F32).T.astype(BF16)
     for jj in range(cols):
         rows = chunk_f32[:, jj * tok : (jj + 1) * tok, :].reshape(tokens, channels).astype(BF16)
-        query[jj] = jnp.dot(rows, wq_ref[...], preferred_element_type=F32).astype(BF16)
-        key[jj] = jnp.dot(rows, wk_ref[...], preferred_element_type=F32).astype(BF16)
         value_t[jj] = lax.dot_general(
             value_w, rows, NT, preferred_element_type=F32
         ).astype(BF16)
-        gate[jj] = jax.nn.sigmoid(
-            jnp.dot(rows, wg_ref[...], preferred_element_type=F32) + gate_bias_ref[...]
-        )
+        joined = jnp.dot(rows, weights_qkg, preferred_element_type=F32)
+        query[jj] = joined[:, :channels].astype(BF16)
+        key[jj] = joined[:, channels : 2 * channels].astype(BF16)
+        gate[jj] = jax.nn.sigmoid(joined[:, 2 * channels :] + gate_bias_ref[...])
     shift_row = (mask_ref[...].astype(F32) - 1.0) * 1000000000.0
-    shift[...] = jnp.broadcast_to(shift_row, (lanes, tokens)).T
+    shift[...] = jnp.broadcast_to(shift_row, (group * lanes, tokens)).T
 
     wait_bytes(bias.at[core, pl.ds(0, rows_count - 1)], plane_rs)
     for n in range(1, rows_count):
         other = bias.at[core, lax.rem(my_row + n, rows_count)]
         send(other, other, core_ss, core_rs, (my_row, my_col + 1 - 2 * core))
 
-    row_head = lax.broadcasted_iota(jnp.int32, (lanes, channels), 0) // query_blk
-    chan_head = lax.broadcasted_iota(jnp.int32, (lanes, channels), 1) // head_dim
-    own_head = row_head == chan_head
-
-    def attend_block(half, z):
-        c = z * cores + half
-        bias_f32 = bias[half, :, z].astype(F32).reshape(tokens, lanes)
-        at = pl.multiple_of(c * query_blk, query_blk)
+    row_head = lax.broadcasted_iota(jnp.int32, (group * lanes, channels), 0) // query_blk
+    chan_head = lax.broadcasted_iota(jnp.int32, (group * lanes, channels), 1) // head_dim
+    own_head = lax.rem(row_head, heads) == chan_head
+
+    def attend_blocks(half, z):
+        bias_f32 = jnp.concatenate(
+            [bias[half, :, z + m].astype(F32).reshape(tokens, lanes) for m in range(group)], axis=1
+        )
+        at = [
+            pl.multiple_of(((z + m) * cores + half) * query_blk, query_blk) for m in range(group)
+        ]
         hidden = []
         for jj in range(cols):
-            q_rows = query[jj, pl.ds(at, query_blk), :].astype(F32)
-            q_heads = jnp.where(
-                own_head, jnp.concatenate([q_rows] * heads, axis=0), 0.0
-            ).astype(BF16)
+            copies = []
+            for m in range(group):
+                copies += [query[jj, pl.ds(at[m], query_blk), :].astype(F32)] * heads
+            q_heads = jnp.where(own_head, jnp.concatenate(copies, axis=0), 0.0).astype(BF16)
             scores = lax.dot_general(key[jj], q_heads, NT, preferred_element_type=F32) * scale
             scores = (scores + bias_f32) + shift[...]
             top = jnp.max(scores, axis=0, keepdims=True)
@@ -210,22 +209,23 @@
             denom = jnp.sum(weights, axis=0, keepdims=True)
             numer = jnp.dot(value_t[jj], weights.astype(BF16), preferred_element_type=F32)
             spread = jnp.where(own_head, (numer * (1.0 / denom)).T, 0.0)
-            attended = spread[:query_blk]
-            for h in range(1, heads):
-                attended = attended + spread[h * query_blk : (h + 1) * query_blk]
-            hidden.append((gate[jj, pl.ds(at, query_blk), :] * attended).astype(BF16))
+            for m in range(group):
+                base = m * lanes
+                attended = spread[base : base + query_blk]
+                for h in range(1, heads):
+                    start = base + h * query_blk
+                    attended = attended + spread[start : start + query_blk]
+                hidden.append((gate[jj, pl.ds(at[m], query_blk), :] * attended).astype(BF16))
         update = (
             jnp.dot(jnp.concatenate(hidden, axis=0), wo_ref[...], preferred_element_type=F32)
             + out_bias_ref[...]
         )
-        for o in range(owners):
-            back_send[c * owners + o] = jnp.concatenate(
-                [
-                    update[jj * query_blk + o * tok : jj * query_blk + (o + 1) * tok]
-                    for jj in range(cols)
-                ],
-                axis=0,
-            ).astype(BF16)
+        for m in range(group):
+            for o in range(owners):
+                starts = [(jj * group + m) * query_blk + o * tok for jj in range(cols)]
+                back_send[((z + m) * cores + half) * owners + o] = jnp.concatenate(
+                    [update[start : start + tok] for start in starts], axis=0
+                ).astype(BF16)
 
     def send_back(half, z):
         for o in range(owners):
@@ -235,18 +235,15 @@
             def _():
                 send(back_send.at[p], back_recv.at[me], back_ss, back_rs, place(p))
 
-    pair_step = 2 if line % 2 == 0 else 1
-
     def attend_half(half):
         def step(n, carry):
-            first = lax.rem(lax.div(my_line, pair_step) + n, line // pair_step) * pair_step
-            for m in range(pair_step):
-                attend_block(half, first + m)
-            for m in range(pair_step):
+            first = lax.rem(lax.div(my_line, group) + n, line // group) * group
+            attend_blocks(half, first)
+            for m in range(group):
                 send_back(half, first + m)
             return carry
 
-        lax.fori_loop(0, line // pair_step, step, 0)
+        lax.fori_loop(0, line // group, step, 0)
 
     attend_half(core)
     wait_bytes(bias.at[1 - core], core_rs)
@@ -277,6 +274,7 @@
     cols = width // devices
     tokens = devices * tok
     lanes = heads * query_blk
+    group = 2 - (cols_count // 2) % 2
     operands = (
         slab,
         pair,
@@ -301,7 +299,6 @@
         scratch_shapes=[vmem(x.shape, x.dtype) for x in operands]
         + [
             vmem((tok * width, channels), F32),
-            vmem((key_blk * query_blk, channels), F32),
             vmem((devices, cols * tok, channels), BF16),
             vmem((devices, cols * tok, channels), BF16),
             vmem((2, rows_count, cols_count // 2, key_blk, lanes), BF16),
@@ -310,7 +307,7 @@
             vmem((cols, tokens, channels), BF16),
             vmem((cols, channels, tokens), BF16),
             vmem((cols, tokens, channels), F32),
-            vmem((tokens, lanes), F32),
+            vmem((tokens, group * lanes), F32),
             vmem((devices, cols * tok, channels), BF16),
             vmem((devices, cols * tok, channels), BF16),
             dma((len(operands),)),

time: 33.6 us -> 34.1 us (1.015)
  Pallas kernels: 31.8 us -> 32.3 us
    pallas_call x1, Pallas kernels: 31.8 us -> 32.3 us  [per_device(): pl.pallas_call(functools.partial(kernel, rows_count, cols_count), out_sha...]
where the time goes in v3:
time: 34.1 us; the launch traced here: 34 us
  Pallas kernels  32.3 us (95%)
  local copies, waits for them, and re-layouts  1.67 us (5%)
    pallas_call x1, Pallas kernels, per_device(): pl.pallas_call(functools.partial(kernel, rows_count, cols_count), out_sha...  32.3 us
    unnamed x1, local copies, waits for them, and re-layouts  1.67 us

profile of v3, /device:TPU:0, one launch (start us, length us, event | category | flops | bytes accessed | tf_op | source)
XLA Modules:
  0.0 34.0 jit_solution(5936121769566503695)
XLA Ops:
  0.0 32.3 %triangle.1 = bf16[8,128,128]{2,1,0:T(8,128)(2,1)} custom-call(bf16[8,128,128]{2,1,0:T(8,128)(2,1)} %refs_0_.1, bf16[64,32,128]{2,1,0:T(8,128)(2,1)} %refs_1_.1, s32[1,256]{1,0:T(1,128)} %bitcast.5, f32[1,128]{1,0:T(1,128)} %bitcast.7, bf16[128,128]{1,0:T(8,128)(2,1)} %refs_4_.1, bf16[128,128]{1,0:T(8,128)(2,1)} %refs_5_.1, bf16[128,128]{1,0:T(8,128)(2,1)} %refs_6_.1, ...), custom_call_target="tpu_custom_call" | custom-call | flops 536870912 | bytes 524288 | tf_op jit(solution)/shard_map/triangle/pallas_call | solution.py:294
  32.3 1.7 %copy.14 = bf16[8,128,128]{2,1,0:T(8,128)(2,1)} copy(bf16[8,128,128]{2,1,0:T(8,128)(2,1)} %triangle.1) | data formatting | bytes 524288

commit v4 on v2

--- a/solution.py
+++ b/solution.py
@@ -39,7 +39,6 @@
     ) = local = refs[13:25]
     (
         slab_f32,
-        pair_f32,
         slab_send,
         slab_recv,
         bias,
@@ -75,6 +74,9 @@
     scale = 1.0 / math.sqrt(head_dim)
     cores = 2
     line = cols_count // cores
+    group = 2 - line % 2
+    phases = 2 - cols % 2
+    per = cols // phases
     my_row, my_col = lax.axis_index("row"), lax.axis_index("col")
     my_line, core = lax.div(my_col, cores), lax.rem(my_col, cores)
     me = my_row * cols_count + my_col
@@ -103,12 +105,27 @@
 
     barrier = pltpu.get_barrier_semaphore()
 
-    def greet(n, carry):
-        p = lax.rem(me + n, devices)
-        pl.semaphore_signal(barrier, inc=1, device_id=place(p), device_id_type=MESH)
-        return carry
-
-    lax.fori_loop(1, devices, greet, 0)
+    def each_peer(act):
+        def step(n, carry):
+            r = lax.rem(my_row + n, rows_count)
+            for m in range(cols_count):
+                c = lax.rem(my_col + m, cols_count)
+                if m:
+                    act(r * cols_count + c, (r, c))
+                else:
+
+                    @pl.when(n > 0)
+                    def _():
+                        act(r * cols_count + c, (r, c))
+
+            return carry
+
+        lax.fori_loop(0, rows_count, step, 0)
+
+    def greet(p, target):
+        pl.semaphore_signal(barrier, inc=1, device_id=target, device_id_type=MESH)
+
+    each_peer(greet)
 
     fetch(0).wait()
     fetch(3).wait()
@@ -116,23 +133,24 @@
     for t in range(tok):
         slab_f32[t * width : (t + 1) * width, :] = normalize(slab_ref[t].astype(F32), gain)
     for p in range(devices):
-        parts = [
-            slab_f32[pl.ds(p * cols + jj, tok, stride=width), :] for jj in range(cols)
-        ]
-        slab_send[p] = jnp.concatenate(parts, axis=0).astype(BF16)
-    slab_recv[me] = slab_send[me]
+        for f in range(phases):
+            starts = [p * cols + f * per + jj for jj in range(per)]
+            parts = [slab_f32[pl.ds(start, tok, stride=width), :] for start in starts]
+            slab_send[f, p] = jnp.concatenate(parts, axis=0).astype(BF16)
+    for f in range(phases):
+        slab_recv[f, me] = slab_send[f, me]
     pl.semaphore_wait(barrier, devices - 1)
 
-    def send_slab(n, carry):
-        p = lax.rem(me + n, devices)
-        send(slab_send.at[p], slab_recv.at[me], slab_ss, slab_rs, place(p))
-        return carry
-
-    lax.fori_loop(1, devices, send_slab, 0)
+    def send_slab(f):
+        def act(p, target):
+            send(slab_send.at[f, p], slab_recv.at[f, me], slab_ss, slab_rs.at[f], target)
+
+        each_peer(act)
+
+    send_slab(0)
 
     fetch(1).wait()
     fetch(9).wait()
-    pair_f32[...] = pair_ref[...].astype(F32).reshape(key_blk * query_blk, channels)
     lane_head = lax.broadcasted_iota(jnp.int32, (heads, lanes), 1) // query_blk
     spread_mat = (lane_head == lax.broadcasted_iota(jnp.int32, (heads, lanes), 0)).astype(F32)
     wide = lax.dot_general(
@@ -140,26 +158,23 @@
         spread_mat.astype(BF16),
         (((0,), (0,)), ((), ())),
         preferred_element_type=F32,
-    )
-    lane_query = lax.rem(lax.broadcasted_iota(jnp.int32, (channels, lanes), 1), query_blk)
-
-    def bias_step(il, total):
-        rows = pair_f32[pl.ds(il, key_blk, stride=query_blk), :]
+    ).astype(BF16)
+    part = 16
+    lane_query = lax.rem(lax.broadcasted_iota(jnp.int32, (part, query_blk, lanes), 2), query_blk)
+    own_query = lane_query == lax.broadcasted_iota(jnp.int32, (part, query_blk, lanes), 1)
+    for k in range(0, key_blk, part):
+        rows = pair_ref[k : k + part].astype(F32).reshape(part * query_blk, channels)
         normed = normalize(rows, gain).astype(BF16)
-        weight = jnp.where(lane_query == il, wide, 0.0).astype(BF16)
-        return total + jnp.dot(normed, weight, preferred_element_type=F32)
-
-    total = lax.fori_loop(
-        0, query_blk, bias_step, jnp.zeros((key_blk, lanes), F32), unroll=8
-    )
-    bias[core, my_row, my_line] = total.astype(BF16)
+        spread = jnp.dot(normed, wide, preferred_element_type=F32)
+        spread = jnp.where(own_query, spread.reshape(part, query_blk, lanes), 0.0)
+        bias[core, my_row, my_line, k : k + part, :] = jnp.sum(spread, axis=1).astype(BF16)
     for n in range(1, line):
         z = lax.rem(my_line + n, line)
         tile = bias.at[core, my_row, my_line]
         send(tile, tile, line_ss, line_rs, (my_row, z * cores + core))
 
-    wait_bytes(slab_recv.at[pl.ds(0, devices - 1)], slab_rs)
-    chunk_f32[...] = slab_recv[...].astype(F32)
+    for f in range(1, phases):
+        send_slab(f)
 
     wait_bytes(bias.at[core, my_row, pl.ds(0, line - 1)], line_rs)
     block = bias.at[core, my_row]
@@ -170,19 +185,26 @@
 
     for i in (2, 4, 5, 6, 7, 8, 10, 11):
         fetch(i).wait()
+    weights_qkg = jnp.concatenate([wq_ref[...], wk_ref[...], wg_ref[...]], axis=1)
     value_w = wv_ref[...].astype(F32).T.astype(BF16)
-    for jj in range(cols):
-        rows = chunk_f32[:, jj * tok : (jj + 1) * tok, :].reshape(tokens, channels).astype(BF16)
-        query[jj] = jnp.dot(rows, wq_ref[...], preferred_element_type=F32).astype(BF16)
-        key[jj] = jnp.dot(rows, wk_ref[...], preferred_element_type=F32).astype(BF16)
-        value_t[jj] = lax.dot_general(
-            value_w, rows, NT, preferred_element_type=F32
-        ).astype(BF16)
-        gate[jj] = jax.nn.sigmoid(
-            jnp.dot(rows, wg_ref[...], preferred_element_type=F32) + gate_bias_ref[...]
-        )
+
+    def project(f):
+        wait_bytes(slab_recv.at[f, pl.ds(0, devices - 1)], slab_rs.at[f])
+        chunk_f32[...] = slab_recv[f].astype(F32)
+        for j in range(per):
+            jj = f * per + j
+            rows = chunk_f32[:, j * tok : (j + 1) * tok, :].reshape(tokens, channels).astype(BF16)
+            value_t[jj] = lax.dot_general(
+                value_w, rows, NT, preferred_element_type=F32
+            ).astype(BF16)
+            joined = jnp.dot(rows, weights_qkg, preferred_element_type=F32)
+            query[jj] = joined[:, :channels].astype(BF16)
+            key[jj] = joined[:, channels : 2 * channels].astype(BF16)
+            gate[jj] = jax.nn.sigmoid(joined[:, 2 * channels :] + gate_bias_ref[...])
+
     shift_row = (mask_ref[...].astype(F32) - 1.0) * 1000000000.0
     shift[...] = jnp.broadcast_to(shift_row, (lanes, tokens)).T
+    project(0)
 
     wait_bytes(bias.at[core, pl.ds(0, rows_count - 1)], plane_rs)
     for n in range(1, rows_count):
@@ -193,12 +215,13 @@
     chan_head = lax.broadcasted_iota(jnp.int32, (lanes, channels), 1) // head_dim
     own_head = row_head == chan_head
 
-    def attend_block(half, z):
+    def attend_block(f, half, z):
         c = z * cores + half
         bias_f32 = bias[half, :, z].astype(F32).reshape(tokens, lanes)
         at = pl.multiple_of(c * query_blk, query_blk)
         hidden = []
-        for jj in range(cols):
+        for j in range(per):
+            jj = f * per + j
             q_rows = query[jj, pl.ds(at, query_blk), :].astype(F32)
             q_heads = jnp.where(
                 own_head, jnp.concatenate([q_rows] * heads, axis=0), 0.0
@@ -219,48 +242,49 @@
             + out_bias_ref[...]
         )
         for o in range(owners):
-            back_send[c * owners + o] = jnp.concatenate(
-                [
-                    update[jj * query_blk + o * tok : jj * query_blk + (o + 1) * tok]
-                    for jj in range(cols)
-                ],
-                axis=0,
+            starts = [j * query_blk + o * tok for j in range(per)]
+            back_send[f, c * owners + o] = jnp.concatenate(
+                [update[start : start + tok] for start in starts], axis=0
             ).astype(BF16)
 
-    def send_back(half, z):
+    def send_back(f, half, z):
         for o in range(owners):
             p = (z * cores + half) * owners + o
 
             @pl.when(p != me)
             def _():
-                send(back_send.at[p], back_recv.at[me], back_ss, back_rs, place(p))
-
-    pair_step = 2 if line % 2 == 0 else 1
-
-    def attend_half(half):
+                send(back_send.at[f, p], back_recv.at[f, me], back_ss, back_rs, place(p))
+
+    def attend_half(f, half):
         def step(n, carry):
-            first = lax.rem(lax.div(my_line, pair_step) + n, line // pair_step) * pair_step
-            for m in range(pair_step):
-                attend_block(half, first + m)
-            for m in range(pair_step):
-                send_back(half, first + m)
+            first = lax.rem(lax.div(my_line, group) + n, line // group) * group
+            for m in range(group):
+                attend_block(f, half, first + m)
+            for m in range(group):
+                send_back(f, half, first + m)
             return carry
 
-        lax.fori_loop(0, line // pair_step, step, 0)
-
-    attend_half(core)
+        lax.fori_loop(0, line // group, step, 0)
+
+    attend_half(0, core)
     wait_bytes(bias.at[1 - core], core_rs)
-    attend_half(1 - core)
-    back_recv[me] = back_send[me]
-
-    wait_bytes(slab_send.at[pl.ds(0, devices - 1)], slab_ss)
+    attend_half(0, 1 - core)
+    for f in range(1, phases):
+        project(f)
+        attend_half(f, core)
+        attend_half(f, 1 - core)
+    for f in range(phases):
+        back_recv[f, me] = back_send[f, me]
+
+    wait_bytes(slab_send.at[:, pl.ds(0, devices - 1)], slab_ss)
     wait_bytes(bias.at[core, my_row, pl.ds(0, line - 1)], line_ss)
     wait_bytes(bias.at[core, pl.ds(0, rows_count - 1)], plane_ss)
     wait_bytes(bias.at[core], core_ss)
-    wait_bytes(back_send.at[pl.ds(0, devices - 1)], back_ss)
-
-    wait_bytes(back_recv.at[pl.ds(0, devices - 1)], back_rs)
-    slab_f32[...] = back_recv[...].astype(F32).reshape(width * tok, channels)
+    wait_bytes(back_send.at[:, pl.ds(0, devices - 1)], back_ss)
+    wait_bytes(back_recv.at[:, pl.ds(0, devices - 1)], back_rs)
+    slab_f32[...] = jnp.stack([back_recv[f] for f in range(phases)], axis=1).astype(F32).reshape(
+        width * tok, channels
+    )
     for t in range(tok):
         out_ref[t] = slab_f32[pl.ds(t, width, stride=tok), :].astype(BF16)
 
@@ -277,6 +301,8 @@
     cols = width // devices
     tokens = devices * tok
     lanes = heads * query_blk
+    phases = 2 - cols % 2
+    rows = cols // phases * tok
     operands = (
         slab,
         pair,
@@ -301,21 +327,21 @@
         scratch_shapes=[vmem(x.shape, x.dtype) for x in operands]
         + [
             vmem((tok * width, channels), F32),
-            vmem((key_blk * query_blk, channels), F32),
-            vmem((devices, cols * tok, channels), BF16),
-            vmem((devices, cols * tok, channels), BF16),
+            vmem((phases, devices, rows, channels), BF16),
+            vmem((phases, devices, rows, channels), BF16),
             vmem((2, rows_count, cols_count // 2, key_blk, lanes), BF16),
-            vmem((devices, cols * tok, channels), F32),
+            vmem((devices, rows, channels), F32),
             vmem((cols, tokens, channels), BF16),
             vmem((cols, tokens, channels), BF16),
             vmem((cols, channels, tokens), BF16),
             vmem((cols, tokens, channels), F32),
             vmem((tokens, lanes), F32),
-            vmem((devices, cols * tok, channels), BF16),
-            vmem((devices, cols * tok, channels), BF16),
+            vmem((phases, devices, rows, channels), BF16),
+            vmem((phases, devices, rows, channels), BF16),
             dma((len(operands),)),
         ]
-        + [dma] * 10,
+        + [dma, dma((phases,))]
+        + [dma] * 8,
         compiler_params=pltpu.CompilerParams(
             collective_id=0, has_side_effects=True, vmem_limit_bytes=56 * 1024 * 1024
         ),

time: 33.6 us -> 34.3 us (1.021)
  Pallas kernels: 31.8 us -> 32.4 us
    pallas_call x1, Pallas kernels: 31.8 us -> 32.4 us  [per_device(): pl.pallas_call(functools.partial(kernel, rows_count, cols_count), out_sha...]
where the time goes in v4:
time: 34.3 us; the launch traced here: 34.1 us
  Pallas kernels  32.4 us (94%)
  local copies, waits for them, and re-layouts  1.67 us (5%)
    pallas_call x1, Pallas kernels, per_device(): pl.pallas_call(functools.partial(kernel, rows_count, cols_count), out_sha...  32.4 us
    unnamed x1, local copies, waits for them, and re-layouts  1.67 us

profile of v4, /device:TPU:0, one launch (start us, length us, event | category | flops | bytes accessed | tf_op | source)
XLA Modules:
  0.0 34.1 jit_solution(2471021172607546637)
XLA Ops:
  0.0 32.4 %triangle.1 = bf16[8,128,128]{2,1,0:T(8,128)(2,1)} custom-call(bf16[8,128,128]{2,1,0:T(8,128)(2,1)} %refs_0_.1, bf16[64,32,128]{2,1,0:T(8,128)(2,1)} %refs_1_.1, s32[1,256]{1,0:T(1,128)} %bitcast.5, f32[1,128]{1,0:T(1,128)} %bitcast.7, bf16[128,128]{1,0:T(8,128)(2,1)} %refs_4_.1, bf16[128,128]{1,0:T(8,128)(2,1)} %refs_5_.1, bf16[128,128]{1,0:T(8,128)(2,1)} %refs_6_.1, ...), custom_call_target="tpu_custom_call" | custom-call | flops 536870912 | bytes 524288 | tf_op jit(solution)/shard_map/triangle/pallas_call | solution.py:322
  32.4 1.7 %copy.14 = bf16[8,128,128]{2,1,0:T(8,128)(2,1)} copy(bf16[8,128,128]{2,1,0:T(8,128)(2,1)} %triangle.1) | data formatting | bytes 524288

commit v5 on v4

--- a/solution.py
+++ b/solution.py
@@ -11,7 +11,6 @@
 MESH = pl.DeviceIdType.MESH
 F32 = jnp.float32
 BF16 = jnp.bfloat16
-NT = (((1,), (1,)), ((), ()))
 
 
 def normalize(values, gain):
@@ -44,10 +43,10 @@
         bias,
         chunk_f32,
         query,
-        key,
-        value_t,
+        key_t,
+        value,
         gate,
-        shift,
+        bias_t,
         back_send,
         back_recv,
         in_sem,
@@ -185,8 +184,7 @@
 
     for i in (2, 4, 5, 6, 7, 8, 10, 11):
         fetch(i).wait()
-    weights_qkg = jnp.concatenate([wq_ref[...], wk_ref[...], wg_ref[...]], axis=1)
-    value_w = wv_ref[...].astype(F32).T.astype(BF16)
+    joined_w = jnp.concatenate([wq_ref[...], wk_ref[...], wv_ref[...], wg_ref[...]], axis=1)
 
     def project(f):
         wait_bytes(slab_recv.at[f, pl.ds(0, devices - 1)], slab_rs.at[f])
@@ -194,16 +192,12 @@
         for j in range(per):
             jj = f * per + j
             rows = chunk_f32[:, j * tok : (j + 1) * tok, :].reshape(tokens, channels).astype(BF16)
-            value_t[jj] = lax.dot_general(
-                value_w, rows, NT, preferred_element_type=F32
-            ).astype(BF16)
-            joined = jnp.dot(rows, weights_qkg, preferred_element_type=F32)
+            joined = jnp.dot(rows, joined_w, preferred_element_type=F32)
             query[jj] = joined[:, :channels].astype(BF16)
-            key[jj] = joined[:, channels : 2 * channels].astype(BF16)
-            gate[jj] = jax.nn.sigmoid(joined[:, 2 * channels :] + gate_bias_ref[...])
-
-    shift_row = (mask_ref[...].astype(F32) - 1.0) * 1000000000.0
-    shift[...] = jnp.broadcast_to(shift_row, (lanes, tokens)).T
+            key_t[jj] = joined[:, channels : 2 * channels].T.astype(BF16)
+            value[jj] = joined[:, 2 * channels : 3 * channels].astype(BF16)
+            gate[jj] = jax.nn.sigmoid(joined[:, 3 * channels :] + gate_bias_ref[...])
+
     project(0)
 
     wait_bytes(bias.at[core, pl.ds(0, rows_count - 1)], plane_rs)
@@ -211,41 +205,59 @@
         other = bias.at[core, lax.rem(my_row + n, rows_count)]
         send(other, other, core_ss, core_rs, (my_row, my_col + 1 - 2 * core))
 
-    row_head = lax.broadcasted_iota(jnp.int32, (lanes, channels), 0) // query_blk
-    chan_head = lax.broadcasted_iota(jnp.int32, (lanes, channels), 1) // head_dim
-    own_head = row_head == chan_head
-
-    def attend_block(f, half, z):
-        c = z * cores + half
-        bias_f32 = bias[half, :, z].astype(F32).reshape(tokens, lanes)
-        at = pl.multiple_of(c * query_blk, query_blk)
+    row_head = lax.broadcasted_iota(jnp.int32, (group * lanes, channels), 0) // query_blk
+    chan_head = lax.broadcasted_iota(jnp.int32, (group * lanes, channels), 1) // head_dim
+    own_head = lax.rem(row_head, heads) == chan_head
+    shift = (mask_ref[...].astype(F32) - 1.0) * 1000000000.0
+
+    def turn_bias(half):
+        def step(z, carry):
+            bias_t[half, z] = bias[half, :, z].astype(F32).reshape(tokens, lanes).T
+            return carry
+
+        lax.fori_loop(0, line, step, 0)
+
+    def attend_blocks(f, half, z):
+        at = [
+            pl.multiple_of(((z + m) * cores + half) * query_blk, query_blk) for m in range(group)
+        ]
+        bias_rows = bias_t[half, pl.ds(z, group)].reshape(group * lanes, tokens)
+        every = range(f * per, f * per + per)
+        scores = []
+        for jj in every:
+            copies = []
+            for m in range(group):
+                copies += [query[jj, pl.ds(at[m], query_blk), :].astype(F32)] * heads
+            q_heads = jnp.where(own_head, jnp.concatenate(copies, axis=0), 0.0).astype(BF16)
+            scores.append(jnp.dot(q_heads, key_t[jj], preferred_element_type=F32))
+        scores = [(x * scale + bias_rows) + shift for x in scores]
+        tops = [jnp.max(x, axis=1, keepdims=True) for x in scores]
+        weights = [jnp.exp(x - top) for x, top in zip(scores, tops)]
+        denoms = [jnp.sum(x, axis=1, keepdims=True) for x in weights]
+        numers = [
+            jnp.dot(x.astype(BF16), value[jj], preferred_element_type=F32)
+            for x, jj in zip(weights, every)
+        ]
         hidden = []
-        for j in range(per):
-            jj = f * per + j
-            q_rows = query[jj, pl.ds(at, query_blk), :].astype(F32)
-            q_heads = jnp.where(
-                own_head, jnp.concatenate([q_rows] * heads, axis=0), 0.0
-            ).astype(BF16)
-            scores = lax.dot_general(key[jj], q_heads, NT, preferred_element_type=F32) * scale
-            scores = (scores + bias_f32) + shift[...]
-            top = jnp.max(scores, axis=0, keepdims=True)
-            weights = jnp.exp(scores - top)
-            denom = jnp.sum(weights, axis=0, keepdims=True)
-            numer = jnp.dot(value_t[jj], weights.astype(BF16), preferred_element_type=F32)
-            spread = jnp.where(own_head, (numer * (1.0 / denom)).T, 0.0)
-            attended = spread[:query_blk]
-            for h in range(1, heads):
-                attended = attended + spread[h * query_blk : (h + 1) * query_blk]
-            hidden.append((gate[jj, pl.ds(at, query_blk), :] * attended).astype(BF16))
+        for numer, denom, jj in zip(numers, denoms, every):
+            spread = jnp.where(own_head, numer * (1.0 / denom), 0.0)
+            for m in range(group):
+                base = m * lanes
+                attended = spread[base : base + query_blk]
+                for h in range(1, heads):
+                    start = base + h * query_blk
+                    attended = attended + spread[start : start + query_blk]
+                hidden.append((gate[jj, pl.ds(at[m], query_blk), :] * attended).astype(BF16))
         update = (
             jnp.dot(jnp.concatenate(hidden, axis=0), wo_ref[...], preferred_element_type=F32)
             + out_bias_ref[...]
         )
-        for o in range(owners):
-            starts = [j * query_blk + o * tok for j in range(per)]
-            back_send[f, c * owners + o] = jnp.concatenate(
-                [update[start : start + tok] for start in starts], axis=0
-            ).astype(BF16)
+        for m in range(group):
+            for o in range(owners):
+                starts = [(j * group + m) * query_blk + o * tok for j in range(per)]
+                back_send[f, ((z + m) * cores + half) * owners + o] = jnp.concatenate(
+                    [update[start : start + tok] for start in starts], axis=0
+                ).astype(BF16)
 
     def send_back(f, half, z):
         for o in range(owners):
@@ -258,16 +270,17 @@
     def attend_half(f, half):
         def step(n, carry):
             first = lax.rem(lax.div(my_line, group) + n, line // group) * group
-            for m in range(group):
-                attend_block(f, half, first + m)
+            attend_blocks(f, half, first)
             for m in range(group):
                 send_back(f, half, first + m)
             return carry
 
         lax.fori_loop(0, line // group, step, 0)
 
+    turn_bias(core)
     attend_half(0, core)
     wait_bytes(bias.at[1 - core], core_rs)
+    turn_bias(1 - core)
     attend_half(0, 1 - core)
     for f in range(1, phases):
         project(f)
@@ -332,10 +345,10 @@
             vmem((2, rows_count, cols_count // 2, key_blk, lanes), BF16),
             vmem((devices, rows, channels), F32),
             vmem((cols, tokens, channels), BF16),
+            vmem((cols, channels, tokens), BF16),
             vmem((cols, tokens, channels), BF16),
-            vmem((cols, channels, tokens), BF16),
             vmem((cols, tokens, channels), F32),
-            vmem((tokens, lanes), F32),
+            vmem((2, cols_count // 2, lanes, tokens), F32),
             vmem((phases, devices, rows, channels), BF16),
             vmem((phases, devices, rows, channels), BF16),
             dma((len(operands),)),

time: 34.3 us -> 31.8 us (0.927)
  Pallas kernels: 32.4 us -> 30 us
    pallas_call x1, Pallas kernels: 32.4 us -> 30 us  [per_device(): pl.pallas_call(functools.partial(kernel, rows_count, cols_count), out_sha...]
where the time goes in v5:
time: 31.8 us; the launch traced here: 31.7 us
  Pallas kernels  30 us (94%)
  local copies, waits for them, and re-layouts  1.67 us (5%)
    pallas_call x1, Pallas kernels, per_device(): pl.pallas_call(functools.partial(kernel, rows_count, cols_count), out_sha...  30 us
    unnamed x1, local copies, waits for them, and re-layouts  1.67 us

profile of v5, /device:TPU:0, one launch (start us, length us, event | category | flops | bytes accessed | tf_op | source)
XLA Modules:
  0.0 31.7 jit_solution(7514060157550121103)
XLA Ops:
  0.0 30.0 %triangle.1 = bf16[8,128,128]{2,1,0:T(8,128)(2,1)} custom-call(bf16[8,128,128]{2,1,0:T(8,128)(2,1)} %refs_0_.1, bf16[64,32,128]{2,1,0:T(8,128)(2,1)} %refs_1_.1, s32[1,256]{1,0:T(1,128)} %bitcast.5, f32[1,128]{1,0:T(1,128)} %bitcast.7, bf16[128,128]{1,0:T(8,128)(2,1)} %refs_4_.1, bf16[128,128]{1,0:T(8,128)(2,1)} %refs_5_.1, bf16[128,128]{1,0:T(8,128)(2,1)} %refs_6_.1, ...), custom_call_target="tpu_custom_call" | custom-call | flops 536870912 | bytes 524288 | tf_op jit(solution)/shard_map/triangle/pallas_call | solution.py:335
  30.0 1.7 %copy.14 = bf16[8,128,128]{2,1,0:T(8,128)(2,1)} copy(bf16[8,128,128]{2,1,0:T(8,128)(2,1)} %triangle.1) | data formatting | bytes 524288

commit v6 on v5

--- a/solution.py
+++ b/solution.py
@@ -74,7 +74,7 @@
     cores = 2
     line = cols_count // cores
     group = 2 - line % 2
-    phases = 2 - cols % 2
+    phases = 1
     per = cols // phases
     my_row, my_col = lax.axis_index("row"), lax.axis_index("col")
     my_line, core = lax.div(my_col, cores), lax.rem(my_col, cores)
@@ -314,7 +314,7 @@
     cols = width // devices
     tokens = devices * tok
     lanes = heads * query_blk
-    phases = 2 - cols % 2
+    phases = 1
     rows = cols // phases * tok
     operands = (
         slab,

time: 31.8 us -> 33 us (1.038)
  Pallas kernels: 30 us -> 31.1 us
    pallas_call x1, Pallas kernels: 30 us -> 31.1 us  [per_device(): pl.pallas_call(functools.partial(kernel, rows_count, cols_count), out_sha...]
where the time goes in v6:
time: 33 us; the launch traced here: 32.8 us
  Pallas kernels  31.1 us (94%)
  local copies, waits for them, and re-layouts  1.67 us (5%)
    pallas_call x1, Pallas kernels, per_device(): pl.pallas_call(functools.partial(kernel, rows_count, cols_count), out_sha...  31.1 us
    unnamed x1, local copies, waits for them, and re-layouts  1.67 us

profile of v6, /device:TPU:0, one launch (start us, length us, event | category | flops | bytes accessed | tf_op | source)
XLA Modules:
  0.0 32.8 jit_solution(15028256554981680830)
XLA Ops:
  0.0 31.1 %triangle.1 = bf16[8,128,128]{2,1,0:T(8,128)(2,1)} custom-call(bf16[8,128,128]{2,1,0:T(8,128)(2,1)} %refs_0_.1, bf16[64,32,128]{2,1,0:T(8,128)(2,1)} %refs_1_.1, s32[1,256]{1,0:T(1,128)} %bitcast.5, f32[1,128]{1,0:T(1,128)} %bitcast.7, bf16[128,128]{1,0:T(8,128)(2,1)} %refs_4_.1, bf16[128,128]{1,0:T(8,128)(2,1)} %refs_5_.1, bf16[128,128]{1,0:T(8,128)(2,1)} %refs_6_.1, ...), custom_call_target="tpu_custom_call" | custom-call | flops 536870912 | bytes 524288 | tf_op jit(solution)/shard_map/triangle/pallas_call | solution.py:335
  31.1 1.7 %copy.14 = bf16[8,128,128]{2,1,0:T(8,128)(2,1)} copy(bf16[8,128,128]{2,1,0:T(8,128)(2,1)} %triangle.1) | data formatting | bytes 524288

commit v7 on v5

--- a/solution.py
+++ b/solution.py
@@ -129,15 +129,17 @@
     fetch(0).wait()
     fetch(3).wait()
     gain = gain_ref[...]
+    flat = slab_f32.reshape(width * tok, channels)
     for t in range(tok):
-        slab_f32[t * width : (t + 1) * width, :] = normalize(slab_ref[t].astype(F32), gain)
-    for p in range(devices):
-        for f in range(phases):
+        flat[t * width : (t + 1) * width, :] = normalize(slab_ref[t].astype(F32), gain)
+    def cut_slab(f):
+        for p in range(devices):
             starts = [p * cols + f * per + jj for jj in range(per)]
-            parts = [slab_f32[pl.ds(start, tok, stride=width), :] for start in starts]
+            parts = [flat[pl.ds(start, tok, stride=width), :] for start in starts]
             slab_send[f, p] = jnp.concatenate(parts, axis=0).astype(BF16)
-    for f in range(phases):
         slab_recv[f, me] = slab_send[f, me]
+
+    cut_slab(0)
     pl.semaphore_wait(barrier, devices - 1)
 
     def send_slab(f):
@@ -173,6 +175,7 @@
         send(tile, tile, line_ss, line_rs, (my_row, z * cores + core))
 
     for f in range(1, phases):
+        cut_slab(f)
         send_slab(f)
 
     wait_bytes(bias.at[core, my_row, pl.ds(0, line - 1)], line_rs)
@@ -265,17 +268,21 @@
 
             @pl.when(p != me)
             def _():
-                send(back_send.at[f, p], back_recv.at[f, me], back_ss, back_rs, place(p))
+                send(back_send.at[f, p], back_recv.at[f, me], back_ss, back_rs.at[f], place(p))
 
     def attend_half(f, half):
-        def step(n, carry):
-            first = lax.rem(lax.div(my_line, group) + n, line // group) * group
-            attend_blocks(f, half, first)
-            for m in range(group):
-                send_back(f, half, first + m)
-            return carry
-
-        lax.fori_loop(0, line // group, step, 0)
+        firsts = [
+            lax.rem(lax.div(my_line, group) + n, line // group) * group
+            for n in range(line // group)
+        ]
+        width_z = min(2, len(firsts))
+        for base in range(0, len(firsts), width_z):
+            some = firsts[base : base + width_z]
+            for first in some:
+                attend_blocks(f, half, first)
+            for first in some:
+                for m in range(group):
+                    send_back(f, half, first + m)
 
     turn_bias(core)
     attend_half(0, core)
@@ -294,12 +301,11 @@
     wait_bytes(bias.at[core, pl.ds(0, rows_count - 1)], plane_ss)
     wait_bytes(bias.at[core], core_ss)
     wait_bytes(back_send.at[:, pl.ds(0, devices - 1)], back_ss)
-    wait_bytes(back_recv.at[:, pl.ds(0, devices - 1)], back_rs)
-    slab_f32[...] = jnp.stack([back_recv[f] for f in range(phases)], axis=1).astype(F32).reshape(
-        width * tok, channels
-    )
+    for f in range(phases):
+        wait_bytes(back_recv.at[f, pl.ds(0, devices - 1)], back_rs.at[f])
+        slab_f32[:, f] = back_recv[f].astype(F32)
     for t in range(tok):
-        out_ref[t] = slab_f32[pl.ds(t, width, stride=tok), :].astype(BF16)
+        out_ref[t] = flat[pl.ds(t, width, stride=tok), :].astype(BF16)
 
 
 def per_device(
@@ -339,7 +345,7 @@
         out_specs=pl.BlockSpec(memory_space=vmem),
         scratch_shapes=[vmem(x.shape, x.dtype) for x in operands]
         + [
-            vmem((tok * width, channels), F32),
+            vmem((devices, phases, rows, channels), F32),
             vmem((phases, devices, rows, channels), BF16),
             vmem((phases, devices, rows, channels), BF16),
             vmem((2, rows_count, cols_count // 2, key_blk, lanes), BF16),
@@ -354,7 +360,8 @@
             dma((len(operands),)),
         ]
         + [dma, dma((phases,))]
-        + [dma] * 8,
+        + [dma] * 7
+        + [dma((phases,))],
         compiler_params=pltpu.CompilerParams(
             collective_id=0, has_side_effects=True, vmem_limit_bytes=56 * 1024 * 1024
         ),

time: 31.8 us -> 32 us (level)
  no operation moved by 1% of the time
where the time goes in v7:
time: 32 us; the launch traced here: 31.8 us
  Pallas kernels  30.2 us (94%)
  local copies, waits for them, and re-layouts  1.67 us (5%)
    pallas_call x1, Pallas kernels, per_device(): pl.pallas_call(functools.partial(kernel, rows_count, cols_count), out_sha...  30.2 us
    unnamed x1, local copies, waits for them, and re-layouts  1.67 us

profile of v7, /device:TPU:0, one launch (start us, length us, event | category | flops | bytes accessed | tf_op | source)
XLA Modules:
  0.0 31.8 jit_solution(4008725027569563675)
XLA Ops:
  0.0 30.2 %triangle.1 = bf16[8,128,128]{2,1,0:T(8,128)(2,1)} custom-call(bf16[8,128,128]{2,1,0:T(8,128)(2,1)} %refs_0_.1, bf16[64,32,128]{2,1,0:T(8,128)(2,1)} %refs_1_.1, s32[1,256]{1,0:T(1,128)} %bitcast.5, f32[1,128]{1,0:T(1,128)} %bitcast.7, bf16[128,128]{1,0:T(8,128)(2,1)} %refs_4_.1, bf16[128,128]{1,0:T(8,128)(2,1)} %refs_5_.1, bf16[128,128]{1,0:T(8,128)(2,1)} %refs_6_.1, ...), custom_call_target="tpu_custom_call" | custom-call | flops 536870912 | bytes 524288 | tf_op jit(solution)/shard_map/triangle/pallas_call | solution.py:341
  30.2 1.7 %copy.14 = bf16[8,128,128]{2,1,0:T(8,128)(2,1)} copy(bf16[8,128,128]{2,1,0:T(8,128)(2,1)} %triangle.1) | data formatting | bytes 524288

commit v8 on v7

--- a/solution.py
+++ b/solution.py
@@ -160,15 +160,18 @@
         (((0,), (0,)), ((), ())),
         preferred_element_type=F32,
     ).astype(BF16)
-    part = 16
+    part, step_k = 4, 16
     lane_query = lax.rem(lax.broadcasted_iota(jnp.int32, (part, query_blk, lanes), 2), query_blk)
     own_query = lane_query == lax.broadcasted_iota(jnp.int32, (part, query_blk, lanes), 1)
-    for k in range(0, key_blk, part):
-        rows = pair_ref[k : k + part].astype(F32).reshape(part * query_blk, channels)
-        normed = normalize(rows, gain).astype(BF16)
-        spread = jnp.dot(normed, wide, preferred_element_type=F32)
-        spread = jnp.where(own_query, spread.reshape(part, query_blk, lanes), 0.0)
-        bias[core, my_row, my_line, k : k + part, :] = jnp.sum(spread, axis=1).astype(BF16)
+    for k in range(0, key_blk, step_k):
+        sums = []
+        for kk in range(k, k + step_k, part):
+            rows = pair_ref[kk : kk + part].astype(F32).reshape(part * query_blk, channels)
+            normed = normalize(rows, gain).astype(BF16)
+            spread = jnp.dot(normed, wide, preferred_element_type=F32)
+            spread = jnp.where(own_query, spread.reshape(part, query_blk, lanes), 0.0)
+            sums.append(jnp.sum(spread, axis=1))
+        bias[core, my_row, my_line, k : k + step_k, :] = jnp.concatenate(sums, axis=0).astype(BF16)
     for n in range(1, line):
         z = lax.rem(my_line + n, line)
         tile = bias.at[core, my_row, my_line]
@@ -233,14 +236,19 @@
                 copies += [query[jj, pl.ds(at[m], query_blk), :].astype(F32)] * heads
             q_heads = jnp.where(own_head, jnp.concatenate(copies, axis=0), 0.0).astype(BF16)
             scores.append(jnp.dot(q_heads, key_t[jj], preferred_element_type=F32))
-        scores = [(x * scale + bias_rows) + shift for x in scores]
-        tops = [jnp.max(x, axis=1, keepdims=True) for x in scores]
-        weights = [jnp.exp(x - top) for x, top in zip(scores, tops)]
-        denoms = [jnp.sum(x, axis=1, keepdims=True) for x in weights]
-        numers = [
-            jnp.dot(x.astype(BF16), value[jj], preferred_element_type=F32)
-            for x, jj in zip(weights, every)
-        ]
+        weights, denoms, numers = [], [], []
+        for x, jj in zip(scores, every):
+            tiles, sums = [], []
+            for start in range(0, group * lanes, query_blk):
+                own = slice(start, start + query_blk)
+                tile = (x[own] * scale + bias_rows[own]) + shift
+                tile = jnp.exp(tile - jnp.max(tile, axis=1, keepdims=True))
+                sums.append(jnp.sum(tile, axis=1, keepdims=True))
+                tiles.append(tile.astype(BF16))
+            weights.append(jnp.concatenate(tiles, axis=0))
+            denoms.append(jnp.concatenate(sums, axis=0))
+        for x, jj in zip(weights, every):
+            numers.append(jnp.dot(x, value[jj], preferred_element_type=F32))
         hidden = []
         for numer, denom, jj in zip(numers, denoms, every):
             spread = jnp.where(own_head, numer * (1.0 / denom), 0.0)
@@ -275,7 +283,7 @@
             lax.rem(lax.div(my_line, group) + n, line // group) * group
             for n in range(line // group)
         ]
-        width_z = min(2, len(firsts))
+        width_z = 1
         for base in range(0, len(firsts), width_z):
             some = firsts[base : base + width_z]
             for first in some:

time: 32 us -> 31.9 us (level)
  no operation moved by 1% of the time
where the time goes in v8:
time: 31.9 us; the launch traced here: 31.7 us
  Pallas kernels  30.1 us (94%)
  local copies, waits for them, and re-layouts  1.67 us (5%)
    pallas_call x1, Pallas kernels, per_device(): pl.pallas_call(functools.partial(kernel, rows_count, cols_count), out_sha...  30.1 us
    unnamed x1, local copies, waits for them, and re-layouts  1.67 us

profile of v8, /device:TPU:0, one launch (start us, length us, event | category | flops | bytes accessed | tf_op | source)
XLA Modules:
  0.0 31.7 jit_solution(351574854173620807)
XLA Ops:
  0.0 30.1 %triangle.1 = bf16[8,128,128]{2,1,0:T(8,128)(2,1)} custom-call(bf16[8,128,128]{2,1,0:T(8,128)(2,1)} %refs_0_.1, bf16[64,32,128]{2,1,0:T(8,128)(2,1)} %refs_1_.1, s32[1,256]{1,0:T(1,128)} %bitcast.5, f32[1,128]{1,0:T(1,128)} %bitcast.7, bf16[128,128]{1,0:T(8,128)(2,1)} %refs_4_.1, bf16[128,128]{1,0:T(8,128)(2,1)} %refs_5_.1, bf16[128,128]{1,0:T(8,128)(2,1)} %refs_6_.1, ...), custom_call_target="tpu_custom_call" | custom-call | flops 536870912 | bytes 524288 | tf_op jit(solution)/shard_map/triangle/pallas_call | solution.py:349
  30.1 1.7 %copy.14 = bf16[8,128,128]{2,1,0:T(8,128)(2,1)} copy(bf16[8,128,128]{2,1,0:T(8,128)(2,1)} %triangle.1) | data formatting | bytes 524288

commit v9 on v8

--- a/solution.py
+++ b/solution.py
@@ -177,16 +177,16 @@
         tile = bias.at[core, my_row, my_line]
         send(tile, tile, line_ss, line_rs, (my_row, z * cores + core))
 
-    for f in range(1, phases):
-        cut_slab(f)
-        send_slab(f)
-
     wait_bytes(bias.at[core, my_row, pl.ds(0, line - 1)], line_rs)
     block = bias.at[core, my_row]
     for n in range(1, rows_count):
         r = lax.rem(my_row + n, rows_count)
         send(block, block, plane_ss, plane_rs, (r, my_col))
     send(block, block, core_ss, core_rs, (my_row, my_col + 1 - 2 * core))
+
+    for f in range(1, phases):
+        cut_slab(f)
+        send_slab(f)
 
     for i in (2, 4, 5, 6, 7, 8, 10, 11):
         fetch(i).wait()

time: 31.9 us -> 31.9 us (level)
  no operation moved by 1% of the time
where the time goes in v9:
time: 31.9 us; the launch traced here: 31.7 us
  Pallas kernels  30.1 us (94%)
  local copies, waits for them, and re-layouts  1.67 us (5%)
    pallas_call x1, Pallas kernels, per_device(): pl.pallas_call(functools.partial(kernel, rows_count, cols_count), out_sha...  30.1 us
    unnamed x1, local copies, waits for them, and re-layouts  1.67 us

profile of v9, /device:TPU:0, one launch (start us, length us, event | category | flops | bytes accessed | tf_op | source)
XLA Modules:
  0.0 31.7 jit_solution(13206632976244799829)
XLA Ops:
  0.0 30.1 %triangle.1 = bf16[8,128,128]{2,1,0:T(8,128)(2,1)} custom-call(bf16[8,128,128]{2,1,0:T(8,128)(2,1)} %refs_0_.1, bf16[64,32,128]{2,1,0:T(8,128)(2,1)} %refs_1_.1, s32[1,256]{1,0:T(1,128)} %bitcast.5, f32[1,128]{1,0:T(1,128)} %bitcast.7, bf16[128,128]{1,0:T(8,128)(2,1)} %refs_4_.1, bf16[128,128]{1,0:T(8,128)(2,1)} %refs_5_.1, bf16[128,128]{1,0:T(8,128)(2,1)} %refs_6_.1, ...), custom_call_target="tpu_custom_call" | custom-call | flops 536870912 | bytes 524288 | tf_op jit(solution)/shard_map/triangle/pallas_call | solution.py:349
  30.1 1.7 %copy.14 = bf16[8,128,128]{2,1,0:T(8,128)(2,1)} copy(bf16[8,128,128]{2,1,0:T(8,128)(2,1)} %triangle.1) | data formatting | bytes 524288
